TPU v7x, 32 devices: a whole 2x2x4 slice. The times are simulated.
32 devices in a mesh: row: 4 (over z), col: 2 (over x), rep: 4 (over y, core).
Axes of the slice: x: 2, y: 2, z: 4, core: 2. Of those that a mesh axis runs over, the one named last changes fastest.
Arguments:
- density: float32 [1024, 1024], P(('col', 'rep'), 'row'), may hold values from -0.25 to 1.25, as said below
- pattern: int32 [16, 9], replicated, may hold values from 0 to 15, as said below
- grid_order: int32 [16], replicated, may hold values from 0 to 15, as said below
Outputs:
- purified: float32 [1024, 1024], P(('col', 'rep'), 'row')
Inputs may be any that keep to these rules, and one draw needn't show every extreme that they name: `pattern`: row r lists (r + d) mod 16 for one set of 9 distinct offsets d that holds 0 and is closed under negation modulo 16. `grid_order`: each block index appears once. `density`: Symmetric; zero outside the blocks that the pattern lists.
All inputs are finite; a program needn't handle non-finite values.
Results may differ from a plain program's by a relative error of at most 0.00016.
Values sent between devices are 32-bit elements; how exact they have to be, the bound alone decides.
No kernel may reach another device: no remote copies, remote signals or barrier semaphores. Data moves between devices by JAX's collectives and lax.ppermute only.
A program may use at most 64 MiB of HBM per device.

v0:
```python
import jax
import jax.numpy as jnp
from jax import lax
from jax.sharding import PartitionSpec as P

BLOCK = 64
STEPS = 2


def block_mask(pattern, grid_order, first_row, first_col, row_blocks, col_blocks):
    total = grid_order.shape[0]
    every = jnp.arange(total, dtype=jnp.int32)
    row_ids = first_row + jnp.arange(row_blocks, dtype=jnp.int32)
    col_ids = first_col + jnp.arange(col_blocks, dtype=jnp.int32)
    row_pick = (row_ids[:, None] == every[None, :]).astype(jnp.int32)
    col_pick = (col_ids[:, None] == every[None, :]).astype(jnp.int32)
    natural_rows = jnp.sum(row_pick * grid_order[None, :], axis=1)
    natural_cols = jnp.sum(col_pick * grid_order[None, :], axis=1)
    row_select = (natural_rows[:, None] == every[None, :]).astype(jnp.int32)
    listed = jnp.sum(row_select[:, :, None] * pattern[None, :, :], axis=1)
    hits = jnp.any(listed[:, :, None] == natural_cols[None, None, :], axis=1)
    return hits.astype(jnp.float32)


def fold_product(left, panel):
    return jnp.dot(
        lax.all_gather(left, "row", axis=1, tiled=True),
        panel,
        precision=lax.Precision.HIGHEST,
        preferred_element_type=jnp.float32,
    )


def local(density, pattern, grid_order):
    row_count, col_count = density.shape
    row_blocks = row_count // BLOCK
    col_blocks = col_count // BLOCK
    first_row = lax.axis_index(("col", "rep")) * row_blocks
    first_col = lax.axis_index("row") * col_blocks
    hits = block_mask(pattern, grid_order, first_row, first_col, row_blocks, col_blocks)
    mask = jnp.broadcast_to(hits[:, None, :, None], (row_blocks, BLOCK, col_blocks, BLOCK)).reshape(
        row_count, col_count
    )
    current = density
    for repeat in range(STEPS):
        panel = lax.all_gather(current, ("col", "rep"), axis=0, tiled=True)
        square = fold_product(current, panel)
        cube = fold_product(square, panel)
        current = mask * (3.0 * square - 2.0 * cube)
    return current


def solution(mesh):
    in_specs = (P(("col", "rep"), "row"), P(), P())
    out_specs = P(("col", "rep"), "row")
    return jax.shard_map(local, mesh=mesh, in_specs=in_specs, out_specs=out_specs, check_vma=False)
```

profile of v0, /device:TPU:0, one launch (start us, length us, event | category | flops | bytes accessed | tf_op | source)
XLA Modules:
  0.0 105.0 jit_solution(8148985976939522087)
XLA Ops:
  6.5 0.0 all-gather.3.cloned.1.call-start
  6.5 0.7 all-gather.3.cloned.1.call-update
  7.3 0.0 all-gather.5.cloned.1.call-start
  7.3 0.0 copy-start.4
  7.3 0.7 copy-done.4
  8.0 0.1 copy.4
  8.1 0.0 copy-start.5
  8.1 0.7 copy-done.5
  8.7 0.2 fusion.4
  8.9 0.1 compare_convert_fusion
  9.0 0.2 multiply_reduce_fusion
  9.3 0.1 copy.5
  9.3 0.2 select_reduce_fusion
  9.5 0.2 compare_reduce_fusion
  9.7 0.1 broadcast_in_dim.2
  9.8 0.0 copy-start.3
  9.9 0.2 reshape.40
  10.1 0.7 copy-done.3
  10.8 17.3 %all_gather.18 = f32[128,1024]{1,0:T(8,128)S(1)} all-gather(f32[128,256]{1,0:T(8,128)S(1)} %copy-done.3), channel_id=1, replica_groups=mesh['row'=4,'col'=2,'rep'=4] {'row'}, dimensions={1}, use_global_device_ids=true | all-gather | bytes 655360 | tf_op jit(solution)/shard_map/all_gather | solution.py:27
  28.1 7.4 %all-gather.3.cloned.1.call-done = f32[1024,256]{1,0:T(8,128)} async-done(((f32[128,256]{1,0:T(8,128)}), f32[1024,256]{1,0:T(8,128)}) %all-gather.3.cloned.1.call-update) | async-done | bytes 1048592 | tf_op jit(solution)/shard_map/all_gather | solution.py:46
  35.5 0.0 copy-start
  35.5 1.9 %fusion.5 = f32[128,256]{1,0:T(8,128)S(1)} fusion(f32[128,1024]{1,0:T(8,128)S(1)} %all_gather.18, f32[1024,256]{1,0:T(8,128)} %all-gather.3.cloned.1.call-done), kind=kOutput, calls=%fused_computation.15 | convolution fusion | flops 402653184 | bytes 1703936 | tf_op jit(solution)/shard_map/dot_general | solution.py:26
  37.4 16.1 %all_gather.20 = f32[128,1024]{1,0:T(8,128)S(1)} all-gather(f32[128,256]{1,0:T(8,128)S(1)} %fusion.5), channel_id=1, replica_groups=mesh['row'=4,'col'=2,'rep'=4] {'row'}, dimensions={1}, use_global_device_ids=true | all-gather | bytes 655360 | tf_op jit(solution)/shard_map/all_gather | solution.py:27
  53.5 0.0 copy-done
  53.5 1.3 %fusion.3 = f32[128,256]{1,0:T(8,128)} fusion(f32[128,256]{1,0:T(8,128)S(1)} %reshape.40, f32[128,1024]{1,0:T(8,128)S(1)} %all_gather.20, f32[1024,256]{1,0:T(8,128)S(1)} %copy-done, f32[128,256]{1,0:T(8,128)S(1)} %fusion.5), kind=kOutput, calls=%fused_computation.5 | convolution fusion | flops 402784256 | bytes 1966080 | tf_op jit(solution)/shard_map/dot_general | solution.py:26
  54.8 0.0 copy-start.2
  54.8 0.0 all-gather.5.cloned.1.call-update
  54.8 0.9 copy-done.2
  55.7 16.0 %all_gather.21 = f32[128,1024]{1,0:T(8,128)S(1)} all-gather(f32[128,256]{1,0:T(8,128)S(1)} %copy-done.2), channel_id=1, replica_groups=mesh['row'=4,'col'=2,'rep'=4] {'row'}, dimensions={1}, use_global_device_ids=true | all-gather | bytes 655360 | tf_op jit(solution)/shard_map/all_gather | solution.py:27
  71.7 7.2 %all-gather.5.cloned.1.call-done = f32[1024,256]{1,0:T(8,128)} async-done(((f32[128,256]{1,0:T(8,128)}), f32[1024,256]{1,0:T(8,128)}) %all-gather.5.cloned.1.call-update) | async-done | bytes 1048592 | tf_op jit(solution)/shard_map/all_gather | solution.py:46
  78.9 0.0 copy-start.1
  78.9 1.9 %fusion.6 = f32[128,256]{1,0:T(8,128)S(1)} fusion(f32[128,1024]{1,0:T(8,128)S(1)} %all_gather.21, f32[1024,256]{1,0:T(8,128)} %all-gather.5.cloned.1.call-done), kind=kOutput, calls=%fused_computation.16 | convolution fusion | flops 402653184 | bytes 1703936 | tf_op jit(solution)/shard_map/dot_general | solution.py:26
  80.8 16.1 %all_gather.23 = f32[128,1024]{1,0:T(8,128)S(1)} all-gather(f32[128,256]{1,0:T(8,128)S(1)} %fusion.6), channel_id=1, replica_groups=mesh['row'=4,'col'=2,'rep'=4] {'row'}, dimensions={1}, use_global_device_ids=true | all-gather | bytes 655360 | tf_op jit(solution)/shard_map/all_gather | solution.py:27
  96.9 0.0 copy-done.1
  96.9 1.3 %fusion.1 = f32[128,256]{1,0:T(8,128)} fusion(f32[128,256]{1,0:T(8,128)S(1)} %reshape.40, f32[128,1024]{1,0:T(8,128)S(1)} %all_gather.23, f32[1024,256]{1,0:T(8,128)S(1)} %copy-done.1, f32[128,256]{1,0:T(8,128)S(1)} %fusion.6), kind=kOutput, calls=%fused_computation.2 | convolution fusion | flops 402784256 | bytes 1966080 | tf_op jit(solution)/shard_map/dot_general | solution.py:26
  (3 shorter events, 0.0 us)
Async XLA Ops:
  6.5 28.9 %all-gather.3.cloned.1.call-start = ((), (), s32[]{:S(2)}) async-start(), calls=%async_computation | async-start | bytes 1179648 | tf_op jit(solution)/shard_map/all_gather | solution.py:46
  7.3 71.6 %all-gather.5.cloned.1.call-start = ((), (), s32[]{:S(2)}) async-start(), calls=%async_computation.1 | async-start | bytes 1179648 | tf_op jit(solution)/shard_map/all_gather | solution.py:46
  7.3 0.7 copy-start.4
  8.1 0.7 copy-start.5
  9.8 0.9 copy-start.3
  35.5 18.0 %copy-start = (f32[1024,256]{1,0:T(8,128)S(1)}, f32[1024,256]{1,0:T(8,128)}, u32[]{:S(2)}) copy-start(f32[1024,256]{1,0:T(8,128)} %all-gather.3.cloned.1.call-done) | copy-start | bytes 3145732
  54.8 0.9 copy-start.2
  78.9 18.0 %copy-start.1 = (f32[1024,256]{1,0:T(8,128)S(1)}, f32[1024,256]{1,0:T(8,128)}, u32[]{:S(2)}) copy-start(f32[1024,256]{1,0:T(8,128)} %all-gather.5.cloned.1.call-done) | copy-start | bytes 3145732
Sparse Core Ops, SparseCore 0:
  9.2 26.1 all-gather.2
  54.9 23.8 all-gather.4
where the time goes:
time: 105 us
  blocking collectives  65.5 us (62%)
  waiting for transfers between devices  15.3 us (15%)
  between operations  13.5 us (13%)
  matrix products  6.49 us (6%)
  local copies, waits for them, and re-layouts  3.4 us (3%)
    all_gather x4, blocking collectives, fold_product(): lax.all_gather(left, 'row', axis=1, tiled=True)  65.5 us
    all_gather x2, waiting for transfers between devices, local(): panel = lax.all_gather(current, ('col', 'rep'), axis=0, tiled=True)  14.5 us
    dot_general x4, matrix products, fold_product(): jnp.dot(lax.all_gather(left, 'row', axis=1, tiled=True), panel, precision...  6.49 us
    unnamed x13, local copies, waits for them, and re-layouts  3 us
  transfers between devices with their start and end apart: 2, of which 2 were waited for; matrix products, arithmetic and copies ran while one was open for 1% of the time, Pallas kernels for 0%

commit v1 on v0

--- a/solution.py
+++ b/solution.py
@@ -1,10 +1,16 @@
+import functools
+
 import jax
 import jax.numpy as jnp
 from jax import lax
+from jax.experimental import pallas as pl
+from jax.experimental.pallas import tpu as pltpu
 from jax.sharding import PartitionSpec as P
 
-BLOCK = 64
 STEPS = 2
+AXES = ("row", "col", "rep")
+VMEM_BYTES = 52 * 2**20
+EXTRA = 8
 
 
 def block_mask(pattern, grid_order, first_row, first_col, row_blocks, col_blocks):
@@ -31,14 +37,14 @@
     )
 
 
-def local(density, pattern, grid_order):
+def panels(block, density, pattern, grid_order):
     row_count, col_count = density.shape
-    row_blocks = row_count // BLOCK
-    col_blocks = col_count // BLOCK
+    row_blocks = row_count // block
+    col_blocks = col_count // block
     first_row = lax.axis_index(("col", "rep")) * row_blocks
     first_col = lax.axis_index("row") * col_blocks
     hits = block_mask(pattern, grid_order, first_row, first_col, row_blocks, col_blocks)
-    mask = jnp.broadcast_to(hits[:, None, :, None], (row_blocks, BLOCK, col_blocks, BLOCK)).reshape(
+    mask = jnp.broadcast_to(hits[:, None, :, None], (row_blocks, block, col_blocks, block)).reshape(
         row_count, col_count
     )
     current = density
@@ -50,7 +56,210 @@
     return current
 
 
+def split(value):
+    high = value.astype(jnp.bfloat16)
+    low = (value - high.astype(jnp.float32)).astype(jnp.bfloat16)
+    return high, low
+
+
+def product(ah, al, bh, bl):
+    dot = functools.partial(jnp.dot, preferred_element_type=jnp.float32)
+    return dot(ah, bh) + (dot(ah, bl) + dot(al, bh))
+
+
+def iotas(side):
+    return (
+        lax.broadcasted_iota(jnp.int32, (side, side), 0),
+        lax.broadcasted_iota(jnp.int32, (side, side), 1),
+    )
+
+
+def pack_kernel(place_ref, x_ref, out_ref):
+    side = x_ref.shape[0]
+    big_row, core, big_col = place_ref[0], place_ref[1], place_ref[2]
+
+    @pl.when(big_row != big_col)
+    def _():
+        pick = jnp.where(big_row < big_col, core, 1 - core)
+        out_ref[:side, :] = x_ref[:, pl.ds(pl.multiple_of(pick * side, side), side)]
+        out_ref[side:, :] = jnp.zeros((EXTRA, side), jnp.float32)
+
+    @pl.when(big_row == big_col)
+    def _():
+        i, j = iotas(side)
+        own = x_ref[:, pl.ds(pl.multiple_of(core * side, side), side)]
+        other = x_ref[:, pl.ds(pl.multiple_of((1 - core) * side, side), side)]
+        out_ref[:side, :] = jnp.where(i >= j, own, other)
+        diagonal = jnp.sum(jnp.where(i == j, other, 0.0), axis=0, keepdims=True)
+        out_ref[side:, :] = jnp.broadcast_to(diagonal, (EXTRA, side))
+
+
+def work_kernel(sizes, place_ref, pattern_ref, order_ref, chunk_ref, out_ref, hits, xh, xl, zh, zl, ch, cl):
+    rows_n, ranks = sizes
+    side = chunk_ref.shape[-1]
+    wide = 2 * side
+    total = xh.shape[0]
+    bigs = total // wide
+    blocks = order_ref.shape[0]
+    block = total // blocks
+    big_row, core, big_col = place_ref[0], place_ref[1], place_ref[2]
+    me = big_col * ranks + big_row * 2 + core
+
+    lane_block = lax.broadcasted_iota(jnp.int32, (blocks, total), 1) // block
+    row_block = lax.broadcasted_iota(jnp.int32, (blocks, total), 0)
+    natural_col = jnp.zeros((blocks, total), jnp.int32)
+    natural_row = jnp.zeros((blocks, total), jnp.int32)
+    for b in range(blocks):
+        natural_col = jnp.where(lane_block == b, order_ref[b], natural_col)
+        natural_row = jnp.where(row_block == b, order_ref[b], natural_row)
+    offset = natural_col - natural_row
+    offset = jnp.where(offset < 0, offset + blocks, offset)
+    hit = jnp.zeros((blocks, total), jnp.bool_)
+    for k in range(pattern_ref.shape[1]):
+        hit = hit | (offset == pattern_ref[0, k])
+    hits[...] = hit.astype(jnp.float32)
+
+    def position(device):
+        away = me ^ device
+        links = (ranks // 2).bit_length() - 1
+        swapped = away & 1
+        order = core ^ swapped
+        spot = away // ranks
+        for step in range(links):
+            bit = jnp.where(order == 0, (away >> (1 + step)) & 1, (away >> (links - step)) & 1)
+            spot = spot + bit * (rows_n << step)
+        return spot + swapped * (rows_n << links)
+
+    def put(h, l, value, r, c):
+        high, low = split(value)
+        h[r, c] = high
+        l[r, c] = low
+
+    def span(index, width):
+        return slice(index * width, (index + 1) * width)
+
+    for a in range(bigs):
+        for b in range(bigs):
+            if a == b:
+                continue
+            for j in range(2):
+                k = j if a < b else 1 - j
+                value = chunk_ref[position(b * ranks + a * 2 + j), :side, :]
+                r, c = span(2 * a + j, side), span(2 * b + k, side)
+                put(xh, xl, value, r, c)
+                put(xh, xl, value.T, c, r)
+    i, j = iotas(side)
+    for a in range(bigs):
+        p0 = position(a * ranks + a * 2)
+        p1 = position(a * ranks + a * 2 + 1)
+        m0 = chunk_ref[p0, :side, :]
+        m1 = chunk_ref[p1, :side, :]
+        diagonal = chunk_ref[p0, side : side + 1, :]
+        t0, t1 = m0.T, m1.T
+        r0, r1 = span(2 * a, side), span(2 * a + 1, side)
+        put(xh, xl, jnp.where(i >= j, m0, t0), r0, r0)
+        put(xh, xl, jnp.where(i >= j, m1, t1), r1, r1)
+        put(xh, xl, jnp.where(i < j, m0, jnp.where(i > j, t1, diagonal)), r0, r1)
+        put(xh, xl, jnp.where(i < j, m1, jnp.where(i > j, t0, diagonal)), r1, r0)
+
+    def masked(value, first_block, cols):
+        parts = []
+        for b in range(value.shape[0] // block):
+            parts.append(value[span(b, block)] * hits[pl.ds(first_block + b, 1), cols])
+        return jnp.concatenate(parts, axis=0)
+
+    for b in range(bigs):
+        r, c = slice(0, (b + 1) * wide), span(b, wide)
+        square = product(xh[r, :], xl[r, :], xh[:, c], xl[:, c])
+        value = 3.0 * (xh[r, c].astype(jnp.float32) + xl[r, c].astype(jnp.float32)) - 2.0 * square
+        put(zh, zl, value, r, c)
+        if b:
+            up = slice(0, b * wide)
+            put(zh, zl, value[up].T, c, up)
+    for b in range(bigs):
+        r, c = slice(0, (b + 1) * wide), span(b, wide)
+        value = masked(product(xh[r, :], xl[r, :], zh[:, c], zl[:, c]), 0, c)
+        put(ch, cl, value, r, c)
+        if b:
+            up = slice(0, b * wide)
+            put(ch, cl, value[up].T, c, up)
+
+    cols = pl.ds(pl.multiple_of(big_col * wide, wide), wide)
+    rows = pl.ds(pl.multiple_of((big_row * 2 + core) * side, side), side)
+    wh, wl = ch[:, cols], cl[:, cols]
+    square = product(ch[...], cl[...], wh, wl)
+    value = 3.0 * (wh.astype(jnp.float32) + wl.astype(jnp.float32)) - 2.0 * square
+    vh, vl = split(value)
+    result = product(ch[rows, :], cl[rows, :], vh, vl)
+    out_ref[...] = masked(result, (big_row * 2 + core) * (side // block), cols)
+
+
+def whole(shape, density, pattern, grid_order):
+    rows_n, cols_n, reps_n = (shape[name] for name in AXES)
+    ranks = cols_n * reps_n
+    side, wide = density.shape
+    total = side * ranks
+
+    def swap(value, partner):
+        pairs = []
+        for z in range(rows_n):
+            for rank in range(ranks):
+                z2, rank2 = partner(z, rank)
+                pairs.append((z * ranks + rank, z2 * ranks + rank2))
+        return lax.ppermute(value, AXES, pairs)
+
+    rank = lax.axis_index(("col", "rep")).astype(jnp.int32)
+    place = jnp.stack([rank // 2, rank % 2, lax.axis_index("row").astype(jnp.int32)])
+    smem = pl.BlockSpec(memory_space=pltpu.SMEM)
+    vmem = pl.BlockSpec(memory_space=pltpu.VMEM)
+    mine = pl.pallas_call(
+        pack_kernel,
+        out_shape=jax.ShapeDtypeStruct((side + EXTRA, side), jnp.float32),
+        in_specs=[smem, vmem],
+        out_specs=vmem,
+        name="pack",
+    )(place, density)
+    parts = [mine[None]]
+    for away in range(1, rows_n):
+        parts.append(swap(mine, lambda z, r, away=away: (z ^ away, r))[None])
+    held = jnp.concatenate(parts, axis=0)
+    links = (ranks // 2).bit_length() - 1
+    for step in range(links):
+        bits = (2 << step, 1 << (links - step))
+        held = jnp.concatenate([held, swap(held, lambda z, r: (z, r ^ bits[r % 2]))], axis=0)
+    held = jnp.concatenate([held, swap(held, lambda z, r: (z, r ^ 1))], axis=0)
+
+    blocks = grid_order.shape[0]
+    bf16 = pltpu.VMEM((total, total), jnp.bfloat16)
+    return pl.pallas_call(
+        functools.partial(work_kernel, (rows_n, ranks)),
+        out_shape=jax.ShapeDtypeStruct((side, wide), jnp.float32),
+        in_specs=[smem, smem, smem, vmem],
+        out_specs=vmem,
+        scratch_shapes=[pltpu.VMEM((blocks, total), jnp.float32)] + [bf16] * 6,
+        compiler_params=pltpu.CompilerParams(vmem_limit_bytes=VMEM_BYTES),
+        name="purify",
+    )(place, pattern, grid_order, held)
+
+
+def fits(shape, side, wide, total):
+    sizes = [shape[name] for name in AXES]
+    powers = all(size & (size - 1) == 0 for size in sizes)
+    ranks = sizes[1] * sizes[2]
+    squares = wide == 2 * side and side % 128 == 0 and sizes[0] * 2 == ranks
+    return powers and squares and total * total * 24 <= VMEM_BYTES // 2 + 2**20
+
+
 def solution(mesh):
     in_specs = (P(("col", "rep"), "row"), P(), P())
     out_specs = P(("col", "rep"), "row")
+    shape = dict(mesh.shape)
+
+    def local(density, pattern, grid_order):
+        side, wide = density.shape
+        total = side * shape["col"] * shape["rep"]
+        if fits(shape, side, wide, total):
+            return whole(shape, density, pattern, grid_order)
+        return panels(total // grid_order.shape[0], density, pattern, grid_order)
+
     return jax.shard_map(local, mesh=mesh, in_specs=in_specs, out_specs=out_specs, check_vma=False)

time: 105 us -> 52.8 us (0.50)
  blocking collectives: 65.5 us -> 0 us
  Pallas kernels: 0 us -> 18.3 us
  between operations: 13.5 us -> 0.09 us
  starting transfers between devices: 0.04 us -> 8.81 us
  matrix products: 6.49 us -> 0 us
  waiting for transfers between devices: 15.3 us -> 21.2 us
    all_gather x4 -> x0, blocking collectives: 65.5 us -> none  [fold_product(): lax.all_gather(left, 'row', axis=1, tiled=True)]
    ppermute x0 -> x6, waiting for transfers between devices: none -> 21.2 us  [swap(): return lax.ppermute(value, AXES, pairs)]
    pallas_call x0 -> x2, Pallas kernels: none -> 18.3 us  [the longest x1 16.7 us: whole(): pl.pallas_call(functools.partial(work_kernel, (rows_n, ranks)), out_shape...]
    all_gather x2 -> x0, waiting for transfers between devices: 14.5 us -> none  [local(): panel = lax.all_gather(current, ('col', 'rep'), axis=0, tiled=True)]
    ppermute x0 -> x6, starting transfers between devices: none -> 8.81 us  [swap(): return lax.ppermute(value, AXES, pairs)]
    dot_general x4 -> x0, matrix products: 6.49 us -> none  [fold_product(): jnp.dot(lax.all_gather(left, 'row', axis=1, tiled=True), panel, precision...]
  transfers between devices with their start and end apart: 2 -> 6, of which waited for: 2 -> 5; matrix products, arithmetic and copies ran while one was open for 1% -> 2% of each run, Pallas kernels for 0% -> 0%
where the time goes in v1:
time: 52.8 us; the launch traced here: 52.5 us
  waiting for transfers between devices  21.2 us (40%)
  Pallas kernels  18.3 us (35%)
  starting transfers between devices  8.81 us (17%)
  local copies, waits for them, and re-layouts  2.59 us (5%)
  other arithmetic  1.54 us (3%)
    ppermute x6, waiting for transfers between devices, swap(): return lax.ppermute(value, AXES, pairs)  21.2 us
    pallas_call x1, Pallas kernels, whole(): pl.pallas_call(functools.partial(work_kernel, (rows_n, ranks)), out_shape...  16.7 us
    ppermute x6, starting transfers between devices, swap(): return lax.ppermute(value, AXES, pairs)  8.81 us
    unnamed x13, local copies, waits for them, and re-layouts  2.44 us
    pallas_call x1, Pallas kernels, whole(): pl.pallas_call(pack_kernel, out_shape=jax.ShapeDtypeStruct((side + EXTRA,...  1.58 us
  transfers between devices with their start and end apart: 6, of which 5 were waited for; matrix products, arithmetic and copies ran while one was open for 2% of the time, Pallas kernels for 0%

profile of v1, /device:TPU:0, one launch (start us, length us, event | category | flops | bytes accessed | tf_op | source)
XLA Modules:
  0.0 52.5 jit_solution(14165411643592220717)
XLA Ops:
  0.0 0.6 %pad_add_fusion.place_ref = s32[3]{0:T(128)} fusion(s32[1]{0:T(128)} %bitcast.2, s32[1]{0:T(128)} %bitcast.1, s32[1]{0:T(128)} %bitcast), kind=kLoop, calls=%fused_computation.19 | loop fusion | flops 6 | bytes 24 | tf_op jit(solution)/shard_map/stack | solution.py:212
  0.6 1.6 %pack.1 = f32[136,128]{1,0:T(8,128)} custom-call(s32[3]{0:T(128)} %pad_add_fusion.place_ref, f32[128,256]{1,0:T(8,128)} %x_ref.1), custom_call_target="tpu_custom_call" | custom-call | tf_op jit(solution)/shard_map/pack/pallas_call | solution.py:215
  2.2 3.0 %collective-permute-start = (f32[136,128]{1,0:T(8,128)}, f32[136,128]{1,0:T(8,128)S(1)}, u32[]{:S(2)}, u32[]{:S(2)}) collective-permute-start(f32[136,128]{1,0:T(8,128)} %pack.1), channel_id=1, source_target_pairs={{0,8},{1,9},{2,10},{3,11},{4,12},{5,13},{6,14},{7,15},{8,0},{9,1},... | collective-permute-start | bytes 208904 | tf_op jit(solution)/shard_map/ppermute | solution.py:209
  5.2 2.6 %collective-permute-start.1 = (f32[136,128]{1,0:T(8,128)}, f32[136,128]{1,0:T(8,128)S(1)}, u32[]{:S(2)}, u32[]{:S(2)}) collective-permute-start(f32[136,128]{1,0:T(8,128)} %pack.1), channel_id=1, source_target_pairs={{0,16},{1,17},{2,18},{3,19},{4,20},{5,21},{6,22},{7,23},{8,24},{9,... | collective-permute-start | bytes 208904 | tf_op jit(solution)/shard_map/ppermute | solution.py:209
  7.8 0.0 collective-permute-start.2
  7.8 1.0 %constant_dynamic-update-slice_fusion.10 = (f32[16,136,128]{2,1,0:T(8,128)S(1)}, f32[8,136,128]{2,1,0:T(8,128)S(1)}, f32[32,136,128]{2,1,0:T(8,128)S(1)}) fusion(f32[136,128]{1,0:T(8,128)} %pack.1), kind=kLoop, calls=%fused_computation.11 | loop fusion | bytes 278528
  8.8 0.0 collective-permute-done
  8.8 4.2 %collective-permute-done.1 = f32[136,128]{1,0:T(8,128)S(1)} collective-permute-done((f32[136,128]{1,0:T(8,128)}, f32[136,128]{1,0:T(8,128)S(1)}, u32[]{:S(2)}, u32[]{:S(2)}) %collective-permute-start.1) | collective-permute-done | bytes 69664 | tf_op jit(solution)/shard_map/ppermute | solution.py:209
  13.0 1.3 %collective-permute-done.2 = f32[136,128]{1,0:T(8,128)S(1)} collective-permute-done((f32[136,128]{1,0:T(8,128)}, f32[136,128]{1,0:T(8,128)S(1)}, u32[]{:S(2)}, u32[]{:S(2)}) %collective-permute-start.2) | collective-permute-done | bytes 69664 | tf_op jit(solution)/shard_map/ppermute | solution.py:209
  14.2 0.9 %pad_maximum_fusion = f32[4,136,128]{2,1,0:T(8,128)S(1)} fusion(f32[1,136,128]{2,1,0:T(8,128)S(1)} %bitcast.20, f32[1,136,128]{2,1,0:T(8,128)S(1)} %bitcast.21, f32[1,136,128]{2,1,0:T(8,128)S(1)} %bitcast.22, f32[1,136,128]{2,1,0:T(8,128)} %bitcast.19), kind=kLoop, calls=%fused_computation | loop fusion | flops 208896 | bytes 557056 | tf_op jit(solution)/shard_map/concatenate | solution.py:225
  15.1 1.6 %collective-permute-start.3 = (f32[4,136,128]{2,1,0:T(8,128)S(1)}, f32[4,136,128]{2,1,0:T(8,128)S(1)}, u32[]{:S(2)}, u32[]{:S(2)}) collective-permute-start(f32[4,136,128]{2,1,0:T(8,128)S(1)} %pad_maximum_fusion), channel_id=1, source_target_pairs={{0,2},{1,5},{2,0},{3,7},{4,6},{5,1},{6,4},{7,3},{8,10},{9,13},{10,... | collective-permute-start | bytes 835592 | tf_op jit(solution)/shard_map/ppermute | solution.py:209
  16.8 5.0 %collective-permute-done.3 = f32[4,136,128]{2,1,0:T(8,128)S(1)} collective-permute-done((f32[4,136,128]{2,1,0:T(8,128)S(1)}, f32[4,136,128]{2,1,0:T(8,128)S(1)}, u32[]{:S(2)}, u32[]{:S(2)}) %collective-permute-start.3) | collective-permute-done | bytes 278560 | tf_op jit(solution)/shard_map/ppermute | solution.py:209
  21.8 0.1 constant_dynamic-update-slice_fusion.6
  21.8 0.0 copy-start
  21.8 0.0 copy-start.1
  21.9 0.0 copy-start.2
  21.9 1.6 %collective-permute-start.4 = (f32[8,136,128]{2,1,0:T(8,128)S(1)}, f32[8,136,128]{2,1,0:T(8,128)S(1)}, u32[]{:S(2)}, u32[]{:S(2)}) collective-permute-start(f32[8,136,128]{2,1,0:T(8,128)S(1)} %get-tuple-element.9), channel_id=1, source_target_pairs={{0,4},{1,3},{2,6},{3,1},{4,0},{5,7},{6,2},{7,5},{8,12},{9,11},{10,... | collective-permute-start | bytes 1671176 | tf_op jit(solution)/shard_map/ppermute | solution.py:209
  23.4 8.0 %collective-permute-done.4 = f32[8,136,128]{2,1,0:T(8,128)S(1)} collective-permute-done((f32[8,136,128]{2,1,0:T(8,128)S(1)}, f32[8,136,128]{2,1,0:T(8,128)S(1)}, u32[]{:S(2)}, u32[]{:S(2)}) %collective-permute-start.4) | collective-permute-done | bytes 557088 | tf_op jit(solution)/shard_map/ppermute | solution.py:209
  31.5 0.1 constant_dynamic-update-slice_fusion.5
  31.5 0.1 collective-permute-start.5
  31.6 2.7 %collective-permute-done.5 = f32[16,136,128]{2,1,0:T(8,128)S(1)} collective-permute-done((f32[16,136,128]{2,1,0:T(8,128)S(1)}, f32[16,136,128]{2,1,0:T(8,128)S(1)}, u32[]{:S(2)}, u32[]{:S(2)}) %collective-permute-start.5) | collective-permute-done | bytes 1114144 | tf_op jit(solution)/shard_map/ppermute | solution.py:209
  34.4 0.1 constant_dynamic-update-slice_fusion.11.chunk_ref
  34.4 0.0 copy-start.3
  34.4 1.4 %copy-done.3 = f32[32,136,128]{2,1,0:T(8,128)} copy-done((f32[32,136,128]{2,1,0:T(8,128)}, f32[32,136,128]{2,1,0:T(8,128)S(1)}, u32[]{:S(2)}) %copy-start.3) | copy-done | bytes 2228248
  35.8 0.0 copy-done
  35.8 0.0 copy-done.1
  35.8 0.0 copy-done.2
  35.8 16.7 %purify.1 = f32[128,256]{1,0:T(8,128)} custom-call(s32[3]{0:T(128)S(1)} %copy-done.1, s32[16,9]{1,0:T(8,128)S(1)} %copy-done, s32[16]{0:T(128)S(1)} %copy-done.2, f32[32,136,128]{2,1,0:T(8,128)} %copy-done.3), custom_call_target="tpu_custom_call" | custom-call | tf_op jit(solution)/shard_map/purify/pallas_call | solution.py:234
  (3 shorter events, 0.0 us)
Async XLA Ops:
  2.2 6.6 %collective-permute-start = (f32[136,128]{1,0:T(8,128)}, f32[136,128]{1,0:T(8,128)S(1)}, u32[]{:S(2)}, u32[]{:S(2)}) collective-permute-start(f32[136,128]{1,0:T(8,128)} %pack.1), channel_id=1, source_target_pairs={{0,8},{1,9},{2,10},{3,11},{4,12},{5,13},{6,14},{7,15},{8,0},{9,1},... | collective-permute-start | bytes 208904 | tf_op jit(solution)/shard_map/ppermute | solution.py:209
  5.2 7.8 %collective-permute-start.1 = (f32[136,128]{1,0:T(8,128)}, f32[136,128]{1,0:T(8,128)S(1)}, u32[]{:S(2)}, u32[]{:S(2)}) collective-permute-start(f32[136,128]{1,0:T(8,128)} %pack.1), channel_id=1, source_target_pairs={{0,16},{1,17},{2,18},{3,19},{4,20},{5,21},{6,22},{7,23},{8,24},{9,... | collective-permute-start | bytes 208904 | tf_op jit(solution)/shard_map/ppermute | solution.py:209
  7.8 6.4 %collective-permute-start.2 = (f32[136,128]{1,0:T(8,128)}, f32[136,128]{1,0:T(8,128)S(1)}, u32[]{:S(2)}, u32[]{:S(2)}) collective-permute-start(f32[136,128]{1,0:T(8,128)} %pack.1), channel_id=1, source_target_pairs={{0,24},{1,25},{2,26},{3,27},{4,28},{5,29},{6,30},{7,31},{8,16},{9,... | collective-permute-start | bytes 208904 | tf_op jit(solution)/shard_map/ppermute | solution.py:209
  15.1 6.6 %collective-permute-start.3 = (f32[4,136,128]{2,1,0:T(8,128)S(1)}, f32[4,136,128]{2,1,0:T(8,128)S(1)}, u32[]{:S(2)}, u32[]{:S(2)}) collective-permute-start(f32[4,136,128]{2,1,0:T(8,128)S(1)} %pad_maximum_fusion), channel_id=1, source_target_pairs={{0,2},{1,5},{2,0},{3,7},{4,6},{5,1},{6,4},{7,3},{8,10},{9,13},{10,... | collective-permute-start | bytes 835592 | tf_op jit(solution)/shard_map/ppermute | solution.py:209
  21.8 14.0 %copy-start = (s32[16,9]{1,0:T(8,128)S(1)}, s32[16,9]{1,0:T(8,128)}, u32[]{:S(2)}) copy-start(s32[16,9]{1,0:T(8,128)} %pattern_ref.1) | copy-start | bytes 1732
  21.8 14.0 %copy-start.1 = (s32[3]{0:T(128)S(1)}, s32[3]{0:T(128)}, u32[]{:S(2)}) copy-start(s32[3]{0:T(128)} %pad_add_fusion.place_ref) | copy-start | bytes 40
  21.9 14.0 %copy-start.2 = (s32[16]{0:T(128)S(1)}, s32[16]{0:T(128)}, u32[]{:S(2)}) copy-start(s32[16]{0:T(128)} %order_ref.1) | copy-start | bytes 196
  21.9 9.6 %collective-permute-start.4 = (f32[8,136,128]{2,1,0:T(8,128)S(1)}, f32[8,136,128]{2,1,0:T(8,128)S(1)}, u32[]{:S(2)}, u32[]{:S(2)}) collective-permute-start(f32[8,136,128]{2,1,0:T(8,128)S(1)} %get-tuple-element.9), channel_id=1, source_target_pairs={{0,4},{1,3},{2,6},{3,1},{4,0},{5,7},{6,2},{7,5},{8,12},{9,11},{10,... | collective-permute-start | bytes 1671176 | tf_op jit(solution)/shard_map/ppermute | solution.py:209
  31.5 2.8 %collective-permute-start.5 = (f32[16,136,128]{2,1,0:T(8,128)S(1)}, f32[16,136,128]{2,1,0:T(8,128)S(1)}, u32[]{:S(2)}, u32[]{:S(2)}) collective-permute-start(f32[16,136,128]{2,1,0:T(8,128)S(1)} %get-tuple-element.5), channel_id=1, source_target_pairs={{0,1},{1,0},{2,3},{3,2},{4,5},{5,4},{6,7},{7,6},{8,9},{9,8},{10,11... | collective-permute-start | bytes 3342344 | tf_op jit(solution)/shard_map/ppermute | solution.py:209
  34.4 1.4 %copy-start.3 = (f32[32,136,128]{2,1,0:T(8,128)}, f32[32,136,128]{2,1,0:T(8,128)S(1)}, u32[]{:S(2)}) copy-start(f32[32,136,128]{2,1,0:T(8,128)S(1)} %constant_dynamic-update-slice_fusion.11.chunk_ref) | copy-start | bytes 6684676

commit v2 on v1

--- a/solution.py
+++ b/solution.py
@@ -9,7 +9,8 @@
 
 STEPS = 2
 AXES = ("row", "col", "rep")
-VMEM_BYTES = 52 * 2**20
+PACK_BYTES = 2 * 2**20
+WORK_BYTES = 28 * 2**20
 EXTRA = 8
 
 
@@ -74,9 +75,14 @@
     )
 
 
-def pack_kernel(place_ref, x_ref, out_ref):
+def place(reps_n):
+    rank = lax.axis_index("col") * reps_n + lax.axis_index("rep")
+    return rank // 2, rank & 1, lax.axis_index("row")
+
+
+def pack_kernel(reps_n, x_ref, out_ref):
     side = x_ref.shape[0]
-    big_row, core, big_col = place_ref[0], place_ref[1], place_ref[2]
+    big_row, core, big_col = place(reps_n)
 
     @pl.when(big_row != big_col)
     def _():
@@ -94,15 +100,15 @@
         out_ref[side:, :] = jnp.broadcast_to(diagonal, (EXTRA, side))
 
 
-def work_kernel(sizes, place_ref, pattern_ref, order_ref, chunk_ref, out_ref, hits, xh, xl, zh, zl, ch, cl):
-    rows_n, ranks = sizes
-    side = chunk_ref.shape[-1]
+def work_kernel(sizes, pattern_ref, order_ref, near_ref, far_ref, out_ref, hits, xh, xl, zh, zl, ch, cl):
+    rows_n, ranks, reps_n = sizes
+    side = near_ref.shape[-1]
     wide = 2 * side
     total = xh.shape[0]
     bigs = total // wide
     blocks = order_ref.shape[0]
     block = total // blocks
-    big_row, core, big_col = place_ref[0], place_ref[1], place_ref[2]
+    big_row, core, big_col = place(reps_n)
     me = big_col * ranks + big_row * 2 + core
 
     lane_block = lax.broadcasted_iota(jnp.int32, (blocks, total), 1) // block
@@ -121,14 +127,19 @@
 
     def position(device):
         away = me ^ device
+        half_n = rows_n // 2
         links = (ranks // 2).bit_length() - 1
         swapped = away & 1
         order = core ^ swapped
-        spot = away // ranks
+        spot = (away // ranks) % half_n
         for step in range(links):
             bit = jnp.where(order == 0, (away >> (1 + step)) & 1, (away >> (links - step)) & 1)
-            spot = spot + bit * (rows_n << step)
-        return spot + swapped * (rows_n << links)
+            spot = spot + bit * (half_n << step)
+        return away // ranks >= half_n, spot + swapped * (half_n << links)
+
+    def chunk(device, rows):
+        far, spot = position(device)
+        return jnp.where(far, far_ref[spot, rows, :], near_ref[spot, rows, :])
 
     def put(h, l, value, r, c):
         high, low = split(value)
@@ -144,17 +155,16 @@
                 continue
             for j in range(2):
                 k = j if a < b else 1 - j
-                value = chunk_ref[position(b * ranks + a * 2 + j), :side, :]
+                value = chunk(b * ranks + a * 2 + j, slice(0, side))
                 r, c = span(2 * a + j, side), span(2 * b + k, side)
                 put(xh, xl, value, r, c)
                 put(xh, xl, value.T, c, r)
     i, j = iotas(side)
     for a in range(bigs):
-        p0 = position(a * ranks + a * 2)
-        p1 = position(a * ranks + a * 2 + 1)
-        m0 = chunk_ref[p0, :side, :]
-        m1 = chunk_ref[p1, :side, :]
-        diagonal = chunk_ref[p0, side : side + 1, :]
+        first = a * ranks + a * 2
+        m0 = chunk(first, slice(0, side))
+        m1 = chunk(first + 1, slice(0, side))
+        diagonal = chunk(first, slice(side, side + 1))
         t0, t1 = m0.T, m1.T
         r0, r1 = span(2 * a, side), span(2 * a + 1, side)
         put(xh, xl, jnp.where(i >= j, m0, t0), r0, r0)
@@ -168,7 +178,7 @@
             parts.append(value[span(b, block)] * hits[pl.ds(first_block + b, 1), cols])
         return jnp.concatenate(parts, axis=0)
 
-    for b in range(bigs):
+    for b in reversed(range(bigs)):
         r, c = slice(0, (b + 1) * wide), span(b, wide)
         square = product(xh[r, :], xl[r, :], xh[:, c], xl[:, c])
         value = 3.0 * (xh[r, c].astype(jnp.float32) + xl[r, c].astype(jnp.float32)) - 2.0 * square
@@ -176,7 +186,13 @@
         if b:
             up = slice(0, b * wide)
             put(zh, zl, value[up].T, c, up)
-    for b in range(bigs):
+    cols = pl.ds(pl.multiple_of(big_col * wide, wide), wide)
+    rank = big_row * 2 + core
+    rows = pl.ds(pl.multiple_of(rank * side, side), side)
+    late = slice(wide, total)
+    for b in reversed(range(bigs)):
+        if b == 0:
+            partial = product(ch[:, late], cl[:, late], ch[late, cols], cl[late, cols])
         r, c = slice(0, (b + 1) * wide), span(b, wide)
         value = masked(product(xh[r, :], xl[r, :], zh[:, c], zl[:, c]), 0, c)
         put(ch, cl, value, r, c)
@@ -184,14 +200,15 @@
             up = slice(0, b * wide)
             put(ch, cl, value[up].T, c, up)
 
-    cols = pl.ds(pl.multiple_of(big_col * wide, wide), wide)
-    rows = pl.ds(pl.multiple_of((big_row * 2 + core) * side, side), side)
-    wh, wl = ch[:, cols], cl[:, cols]
-    square = product(ch[...], cl[...], wh, wl)
-    value = 3.0 * (wh.astype(jnp.float32) + wl.astype(jnp.float32)) - 2.0 * square
-    vh, vl = split(value)
-    result = product(ch[rows, :], cl[rows, :], vh, vl)
-    out_ref[...] = masked(result, (big_row * 2 + core) * (side // block), cols)
+    first = slice(0, wide)
+    result = jnp.zeros((side, wide), jnp.float32)
+    for b in range(bigs):
+        r = span(b, wide)
+        square = partial[r] + product(ch[r, first], cl[r, first], ch[first, cols], cl[first, cols])
+        value = 3.0 * (ch[r, cols].astype(jnp.float32) + cl[r, cols].astype(jnp.float32)) - 2.0 * square
+        vh, vl = split(value)
+        result = result + product(ch[rows, r], cl[rows, r], vh, vl)
+    out_ref[...] = masked(result, rank * (side // block), cols)
 
 
 def whole(shape, density, pattern, grid_order):
@@ -208,38 +225,39 @@
                 pairs.append((z * ranks + rank, z2 * ranks + rank2))
         return lax.ppermute(value, AXES, pairs)
 
-    rank = lax.axis_index(("col", "rep")).astype(jnp.int32)
-    place = jnp.stack([rank // 2, rank % 2, lax.axis_index("row").astype(jnp.int32)])
     smem = pl.BlockSpec(memory_space=pltpu.SMEM)
     vmem = pl.BlockSpec(memory_space=pltpu.VMEM)
     mine = pl.pallas_call(
-        pack_kernel,
+        functools.partial(pack_kernel, reps_n),
         out_shape=jax.ShapeDtypeStruct((side + EXTRA, side), jnp.float32),
-        in_specs=[smem, vmem],
+        in_specs=[vmem],
         out_specs=vmem,
+        compiler_params=pltpu.CompilerParams(vmem_limit_bytes=PACK_BYTES),
         name="pack",
-    )(place, density)
+    )(density)
     parts = [mine[None]]
     for away in range(1, rows_n):
         parts.append(swap(mine, lambda z, r, away=away: (z ^ away, r))[None])
-    held = jnp.concatenate(parts, axis=0)
     links = (ranks // 2).bit_length() - 1
-    for step in range(links):
-        bits = (2 << step, 1 << (links - step))
-        held = jnp.concatenate([held, swap(held, lambda z, r: (z, r ^ bits[r % 2]))], axis=0)
-    held = jnp.concatenate([held, swap(held, lambda z, r: (z, r ^ 1))], axis=0)
+    held = []
+    for half in (parts[: rows_n // 2], parts[rows_n // 2 :]):
+        value = jnp.concatenate(half, axis=0)
+        for step in range(links):
+            bits = (2 << step, 1 << (links - step))
+            value = jnp.concatenate([value, swap(value, lambda z, r: (z, r ^ bits[r % 2]))], axis=0)
+        held.append(jnp.concatenate([value, swap(value, lambda z, r: (z, r ^ 1))], axis=0))
 
     blocks = grid_order.shape[0]
     bf16 = pltpu.VMEM((total, total), jnp.bfloat16)
     return pl.pallas_call(
-        functools.partial(work_kernel, (rows_n, ranks)),
+        functools.partial(work_kernel, (rows_n, ranks, reps_n)),
         out_shape=jax.ShapeDtypeStruct((side, wide), jnp.float32),
-        in_specs=[smem, smem, smem, vmem],
+        in_specs=[smem, smem, vmem, vmem],
         out_specs=vmem,
         scratch_shapes=[pltpu.VMEM((blocks, total), jnp.float32)] + [bf16] * 6,
-        compiler_params=pltpu.CompilerParams(vmem_limit_bytes=VMEM_BYTES),
+        compiler_params=pltpu.CompilerParams(vmem_limit_bytes=WORK_BYTES),
         name="purify",
-    )(place, pattern, grid_order, held)
+    )(pattern, grid_order, *held)
 
 
 def fits(shape, side, wide, total):
@@ -247,7 +265,7 @@
     powers = all(size & (size - 1) == 0 for size in sizes)
     ranks = sizes[1] * sizes[2]
     squares = wide == 2 * side and side % 128 == 0 and sizes[0] * 2 == ranks
-    return powers and squares and total * total * 24 <= VMEM_BYTES // 2 + 2**20
+    return powers and squares and total * total * 24 <= WORK_BYTES
 
 
 def solution(mesh):

time: 52.8 us -> 43.1 us (0.82)
  waiting for transfers between devices: 21.2 us -> 15.7 us
  Pallas kernels: 18.3 us -> 14.7 us
  starting transfers between devices: 8.81 us -> 11.2 us
  local copies, waits for them, and re-layouts: 2.59 us -> 1.08 us
  other arithmetic: 1.54 us -> 0.16 us
    ppermute x6 -> x9, waiting for transfers between devices: 21.2 us -> 15.7 us  [swap(): return lax.ppermute(value, AXES, pairs)]
    pallas_call x2, Pallas kernels: 18.3 us -> 14.7 us  [the longest x1 14.7 us: whole(): pl.pallas_call(functools.partial(work_kernel, (rows_n, ranks, reps_n)), o...]
    ppermute x6 -> x9, starting transfers between devices: 8.81 us -> 11.2 us  [swap(): return lax.ppermute(value, AXES, pairs)]
    unnamed x13 -> x14, local copies, waits for them, and re-layouts: 2.44 us -> 1.01 us
    concatenate x1 -> x6, other arithmetic: 0.91 us -> 0.16 us  [the longest x4 0.13 us: whole(): jnp.concatenate([value, swap(value, lambda z, r: (z, r ^ bits[r % 2]))],...]
    another operation x1 -> x0, other arithmetic: 0.64 us -> none  [whole(): jnp.stack([rank // 2, rank % 2, lax.axis_index('row').astype(jnp.int32)])]
  transfers between devices with their start and end apart: 6 -> 9, of which waited for: 5 -> 7; matrix products, arithmetic and copies ran while one was open for 2% -> 1% of each run, Pallas kernels for 0% -> 0%
where the time goes in v2:
time: 43.1 us; the launch traced here: 43 us
  waiting for transfers between devices  15.7 us (36%)
  Pallas kernels  14.7 us (34%)
  starting transfers between devices  11.2 us (26%)
  local copies, waits for them, and re-layouts  1.08 us (3%)
    ppermute x9, waiting for transfers between devices, swap(): return lax.ppermute(value, AXES, pairs)  15.7 us
    pallas_call x1, Pallas kernels, whole(): pl.pallas_call(functools.partial(work_kernel, (rows_n, ranks, reps_n)), o...  14.7 us
    ppermute x9, starting transfers between devices, swap(): return lax.ppermute(value, AXES, pairs)  11.2 us
    unnamed x14, local copies, waits for them, and re-layouts  1.01 us
  transfers between devices with their start and end apart: 9, of which 7 were waited for; matrix products, arithmetic and copies ran while one was open for 1% of the time, Pallas kernels for 0%

profile of v2, /device:TPU:0, one launch (start us, length us, event | category | flops | bytes accessed | tf_op | source)
XLA Modules:
  0.0 43.0 jit_solution(7955388296826238837)
XLA Ops:
  0.0 0.0 copy-start
  0.0 0.9 %copy-done = f32[128,256]{1,0:T(8,128)S(1)} copy-done((f32[128,256]{1,0:T(8,128)S(1)}, f32[128,256]{1,0:T(8,128)}, u32[]{:S(2)}) %copy-start) | copy-done | bytes 131096
  0.9 4.0 %collective-permute-start.4 = (f32[136,128]{1,0:T(8,128)S(1)}, f32[136,128]{1,0:T(8,128)S(1)}, u32[]{:S(2)}, u32[]{:S(2)}) collective-permute-start(f32[136,128]{1,0:T(8,128)S(1)} %pack.1), channel_id=1, source_target_pairs={{0,16},{1,17},{2,18},{3,19},{4,20},{5,21},{6,22},{7,23},{8,24},{9,... | collective-permute-start | bytes 208904 | tf_op jit(solution)/shard_map/ppermute | solution.py:226
  4.9 1.3 %collective-permute-start.5 = (f32[136,128]{1,0:T(8,128)S(1)}, f32[136,128]{1,0:T(8,128)S(1)}, u32[]{:S(2)}, u32[]{:S(2)}) collective-permute-start(f32[136,128]{1,0:T(8,128)S(1)} %pack.1), channel_id=1, source_target_pairs={{0,24},{1,25},{2,26},{3,27},{4,28},{5,29},{6,30},{7,31},{8,16},{9,... | collective-permute-start | bytes 208904 | tf_op jit(solution)/shard_map/ppermute | solution.py:226
  6.3 0.2 collective-permute-start
  6.5 2.3 %collective-permute-done.4 = f32[136,128]{1,0:T(8,128)S(1)} collective-permute-done((f32[136,128]{1,0:T(8,128)S(1)}, f32[136,128]{1,0:T(8,128)S(1)}, u32[]{:S(2)}, u32[]{:S(2)}) %collective-permute-start.4) | collective-permute-done | bytes 69664 | tf_op jit(solution)/shard_map/ppermute | solution.py:226
  8.8 2.5 %collective-permute-done.5 = f32[136,128]{1,0:T(8,128)S(1)} collective-permute-done((f32[136,128]{1,0:T(8,128)S(1)}, f32[136,128]{1,0:T(8,128)S(1)}, u32[]{:S(2)}, u32[]{:S(2)}) %collective-permute-start.5) | collective-permute-done | bytes 69664 | tf_op jit(solution)/shard_map/ppermute | solution.py:226
  11.3 1.6 %collective-permute-start.6 = (f32[2,136,128]{2,1,0:T(8,128)S(1)}, f32[2,136,128]{2,1,0:T(8,128)S(1)}, u32[]{:S(2)}, u32[]{:S(2)}) collective-permute-start(f32[2,136,128]{2,1,0:T(8,128)S(1)} %pad_maximum_fusion.5), channel_id=1, source_target_pairs={{0,2},{1,5},{2,0},{3,7},{4,6},{5,1},{6,4},{7,3},{8,10},{9,13},{10,... | collective-permute-start | bytes 417800 | tf_op jit(solution)/shard_map/ppermute | solution.py:226
  12.9 0.0 collective-permute-done
  12.9 0.6 %collective-permute-start.1 = (f32[2,136,128]{2,1,0:T(8,128)S(1)}, f32[2,136,128]{2,1,0:T(8,128)S(1)}, u32[]{:S(2)}, u32[]{:S(2)}) collective-permute-start(f32[2,136,128]{2,1,0:T(8,128)S(1)} %pad_maximum_fusion.4), channel_id=1, source_target_pairs={{0,2},{1,5},{2,0},{3,7},{4,6},{5,1},{6,4},{7,3},{8,10},{9,13},{10,... | collective-permute-start | bytes 417800 | tf_op jit(solution)/shard_map/ppermute | solution.py:226
  13.5 3.1 %collective-permute-done.6 = f32[2,136,128]{2,1,0:T(8,128)S(1)} collective-permute-done((f32[2,136,128]{2,1,0:T(8,128)S(1)}, f32[2,136,128]{2,1,0:T(8,128)S(1)}, u32[]{:S(2)}, u32[]{:S(2)}) %collective-permute-start.6) | collective-permute-done | bytes 139296 | tf_op jit(solution)/shard_map/ppermute | solution.py:226
  16.6 1.7 %collective-permute-start.7 = (f32[4,136,128]{2,1,0:T(8,128)S(1)}, f32[4,136,128]{2,1,0:T(8,128)S(1)}, u32[]{:S(2)}, u32[]{:S(2)}) collective-permute-start(f32[4,136,128]{2,1,0:T(8,128)S(1)} %pad_maximum_fusion.3), channel_id=1, source_target_pairs={{0,4},{1,3},{2,6},{3,1},{4,0},{5,7},{6,2},{7,5},{8,12},{9,11},{10,... | collective-permute-start | bytes 835592 | tf_op jit(solution)/shard_map/ppermute | solution.py:226
  18.3 1.3 %collective-permute-done.1 = f32[2,136,128]{2,1,0:T(8,128)S(1)} collective-permute-done((f32[2,136,128]{2,1,0:T(8,128)S(1)}, f32[2,136,128]{2,1,0:T(8,128)S(1)}, u32[]{:S(2)}, u32[]{:S(2)}) %collective-permute-start.1) | collective-permute-done | bytes 139296 | tf_op jit(solution)/shard_map/ppermute | solution.py:226
  19.6 1.7 %collective-permute-start.2 = (f32[4,136,128]{2,1,0:T(8,128)S(1)}, f32[4,136,128]{2,1,0:T(8,128)S(1)}, u32[]{:S(2)}, u32[]{:S(2)}) collective-permute-start(f32[4,136,128]{2,1,0:T(8,128)S(1)} %pad_maximum_fusion.2), channel_id=1, source_target_pairs={{0,4},{1,3},{2,6},{3,1},{4,0},{5,7},{6,2},{7,5},{8,12},{9,11},{10,... | collective-permute-start | bytes 835592 | tf_op jit(solution)/shard_map/ppermute | solution.py:226
  21.3 1.9 %collective-permute-done.7 = f32[4,136,128]{2,1,0:T(8,128)S(1)} collective-permute-done((f32[4,136,128]{2,1,0:T(8,128)S(1)}, f32[4,136,128]{2,1,0:T(8,128)S(1)}, u32[]{:S(2)}, u32[]{:S(2)}) %collective-permute-start.7) | collective-permute-done | bytes 278560 | tf_op jit(solution)/shard_map/ppermute | solution.py:226
  23.2 0.1 pad_maximum_fusion.1
  23.3 0.1 collective-permute-start.8
  23.4 2.9 %collective-permute-done.2 = f32[4,136,128]{2,1,0:T(8,128)S(1)} collective-permute-done((f32[4,136,128]{2,1,0:T(8,128)S(1)}, f32[4,136,128]{2,1,0:T(8,128)S(1)}, u32[]{:S(2)}, u32[]{:S(2)}) %collective-permute-start.2) | collective-permute-done | bytes 278560 | tf_op jit(solution)/shard_map/ppermute | solution.py:226
  26.3 0.1 collective-permute-start.3
  26.4 0.0 copy-start.1
  26.5 0.0 copy-start.2
  26.5 0.0 collective-permute-done.8
  26.5 1.8 %collective-permute-done.3 = f32[8,136,128]{2,1,0:T(8,128)S(1)} collective-permute-done((f32[8,136,128]{2,1,0:T(8,128)S(1)}, f32[8,136,128]{2,1,0:T(8,128)S(1)}, u32[]{:S(2)}, u32[]{:S(2)}) %collective-permute-start.3) | collective-permute-done | bytes 557088 | tf_op jit(solution)/shard_map/ppermute | solution.py:226
  28.3 0.0 copy-done.1
  28.3 0.0 copy-done.2
  28.3 14.7 %purify.1 = f32[128,256]{1,0:T(8,128)} custom-call(s32[16,9]{1,0:T(8,128)S(1)} %copy-done.1, s32[16]{0:T(128)S(1)} %copy-done.2, f32[16,136,128]{2,1,0:T(8,128)S(1)} %constant_dynamic-update-slice_fusion.near_ref, f32[16,136,128]{2,1,0:T(8,128)S(1)} %constant_dynamic-update-slice_fusion.5.far_ref), custom_call_target="tpu_custom_call" | custom-call | tf_op jit(solution)/shard_map/purify/pallas_call | solution.py:252
  (16 shorter events, 0.3 us)
Async XLA Ops:
  0.0 0.9 %copy-start = (f32[128,256]{1,0:T(8,128)S(1)}, f32[128,256]{1,0:T(8,128)}, u32[]{:S(2)}) copy-start(f32[128,256]{1,0:T(8,128)} %x_ref.1) | copy-start | bytes 393220
  0.9 7.9 %collective-permute-start.4 = (f32[136,128]{1,0:T(8,128)S(1)}, f32[136,128]{1,0:T(8,128)S(1)}, u32[]{:S(2)}, u32[]{:S(2)}) collective-permute-start(f32[136,128]{1,0:T(8,128)S(1)} %pack.1), channel_id=1, source_target_pairs={{0,16},{1,17},{2,18},{3,19},{4,20},{5,21},{6,22},{7,23},{8,24},{9,... | collective-permute-start | bytes 208904 | tf_op jit(solution)/shard_map/ppermute | solution.py:226
  4.9 6.3 %collective-permute-start.5 = (f32[136,128]{1,0:T(8,128)S(1)}, f32[136,128]{1,0:T(8,128)S(1)}, u32[]{:S(2)}, u32[]{:S(2)}) collective-permute-start(f32[136,128]{1,0:T(8,128)S(1)} %pack.1), channel_id=1, source_target_pairs={{0,24},{1,25},{2,26},{3,27},{4,28},{5,29},{6,30},{7,31},{8,16},{9,... | collective-permute-start | bytes 208904 | tf_op jit(solution)/shard_map/ppermute | solution.py:226
  6.3 6.6 %collective-permute-start = (f32[136,128]{1,0:T(8,128)S(1)}, f32[136,128]{1,0:T(8,128)S(1)}, u32[]{:S(2)}, u32[]{:S(2)}) collective-permute-start(f32[136,128]{1,0:T(8,128)S(1)} %pack.1), channel_id=1, source_target_pairs={{0,8},{1,9},{2,10},{3,11},{4,12},{5,13},{6,14},{7,15},{8,0},{9,1},... | collective-permute-start | bytes 208904 | tf_op jit(solution)/shard_map/ppermute | solution.py:226
  11.3 5.3 %collective-permute-start.6 = (f32[2,136,128]{2,1,0:T(8,128)S(1)}, f32[2,136,128]{2,1,0:T(8,128)S(1)}, u32[]{:S(2)}, u32[]{:S(2)}) collective-permute-start(f32[2,136,128]{2,1,0:T(8,128)S(1)} %pad_maximum_fusion.5), channel_id=1, source_target_pairs={{0,2},{1,5},{2,0},{3,7},{4,6},{5,1},{6,4},{7,3},{8,10},{9,13},{10,... | collective-permute-start | bytes 417800 | tf_op jit(solution)/shard_map/ppermute | solution.py:226
  12.9 6.7 %collective-permute-start.1 = (f32[2,136,128]{2,1,0:T(8,128)S(1)}, f32[2,136,128]{2,1,0:T(8,128)S(1)}, u32[]{:S(2)}, u32[]{:S(2)}) collective-permute-start(f32[2,136,128]{2,1,0:T(8,128)S(1)} %pad_maximum_fusion.4), channel_id=1, source_target_pairs={{0,2},{1,5},{2,0},{3,7},{4,6},{5,1},{6,4},{7,3},{8,10},{9,13},{10,... | collective-permute-start | bytes 417800 | tf_op jit(solution)/shard_map/ppermute | solution.py:226
  16.6 6.6 %collective-permute-start.7 = (f32[4,136,128]{2,1,0:T(8,128)S(1)}, f32[4,136,128]{2,1,0:T(8,128)S(1)}, u32[]{:S(2)}, u32[]{:S(2)}) collective-permute-start(f32[4,136,128]{2,1,0:T(8,128)S(1)} %pad_maximum_fusion.3), channel_id=1, source_target_pairs={{0,4},{1,3},{2,6},{3,1},{4,0},{5,7},{6,2},{7,5},{8,12},{9,11},{10,... | collective-permute-start | bytes 835592 | tf_op jit(solution)/shard_map/ppermute | solution.py:226
  19.6 6.6 %collective-permute-start.2 = (f32[4,136,128]{2,1,0:T(8,128)S(1)}, f32[4,136,128]{2,1,0:T(8,128)S(1)}, u32[]{:S(2)}, u32[]{:S(2)}) collective-permute-start(f32[4,136,128]{2,1,0:T(8,128)S(1)} %pad_maximum_fusion.2), channel_id=1, source_target_pairs={{0,4},{1,3},{2,6},{3,1},{4,0},{5,7},{6,2},{7,5},{8,12},{9,11},{10,... | collective-permute-start | bytes 835592 | tf_op jit(solution)/shard_map/ppermute | solution.py:226
  23.3 3.2 %collective-permute-start.8 = (f32[8,136,128]{2,1,0:T(8,128)S(1)}, f32[8,136,128]{2,1,0:T(8,128)S(1)}, u32[]{:S(2)}, u32[]{:S(2)}) collective-permute-start(f32[8,136,128]{2,1,0:T(8,128)S(1)} %pad_maximum_fusion.1), channel_id=1, source_target_pairs={{0,1},{1,0},{2,3},{3,2},{4,5},{5,4},{6,7},{7,6},{8,9},{9,8},{10,11... | collective-permute-start | bytes 1671176 | tf_op jit(solution)/shard_map/ppermute | solution.py:226
  26.3 2.0 %collective-permute-start.3 = (f32[8,136,128]{2,1,0:T(8,128)S(1)}, f32[8,136,128]{2,1,0:T(8,128)S(1)}, u32[]{:S(2)}, u32[]{:S(2)}) collective-permute-start(f32[8,136,128]{2,1,0:T(8,128)S(1)} %pad_maximum_fusion), channel_id=1, source_target_pairs={{0,1},{1,0},{2,3},{3,2},{4,5},{5,4},{6,7},{7,6},{8,9},{9,8},{10,11... | collective-permute-start | bytes 1671176 | tf_op jit(solution)/shard_map/ppermute | solution.py:226
  26.4 1.9 %copy-start.1 = (s32[16,9]{1,0:T(8,128)S(1)}, s32[16,9]{1,0:T(8,128)}, u32[]{:S(2)}) copy-start(s32[16,9]{1,0:T(8,128)} %pattern_ref.1) | copy-start | bytes 1732
  26.5 1.9 %copy-start.2 = (s32[16]{0:T(128)S(1)}, s32[16]{0:T(128)}, u32[]{:S(2)}) copy-start(s32[16]{0:T(128)} %order_ref.1) | copy-start | bytes 196

commit v3 on v2

--- a/solution.py
+++ b/solution.py
@@ -64,8 +64,9 @@
 
 
 def product(ah, al, bh, bl):
-    dot = functools.partial(jnp.dot, preferred_element_type=jnp.float32)
-    return dot(ah, bh) + (dot(ah, bl) + dot(al, bh))
+    left = jnp.concatenate([ah, ah, al], axis=1)
+    right = jnp.concatenate([bh, bl, bh], axis=0)
+    return jnp.dot(left, right, preferred_element_type=jnp.float32)
 
 
 def iotas(side):
@@ -100,46 +101,46 @@
         out_ref[side:, :] = jnp.broadcast_to(diagonal, (EXTRA, side))
 
 
-def work_kernel(sizes, pattern_ref, order_ref, near_ref, far_ref, out_ref, hits, xh, xl, zh, zl, ch, cl):
-    rows_n, ranks, reps_n = sizes
-    side = near_ref.shape[-1]
-    wide = 2 * side
-    total = xh.shape[0]
-    bigs = total // wide
-    blocks = order_ref.shape[0]
-    block = total // blocks
-    big_row, core, big_col = place(reps_n)
-    me = big_col * ranks + big_row * 2 + core
-
-    lane_block = lax.broadcasted_iota(jnp.int32, (blocks, total), 1) // block
-    row_block = lax.broadcasted_iota(jnp.int32, (blocks, total), 0)
-    natural_col = jnp.zeros((blocks, total), jnp.int32)
-    natural_row = jnp.zeros((blocks, total), jnp.int32)
+def write_mask(pattern_ref, order_ref, hits):
+    blocks, total = hits.shape
+    lane_block = lax.broadcasted_iota(jnp.int32, (1, total), 1) // (total // blocks)
+    row_block = lax.broadcasted_iota(jnp.int32, (blocks, 1), 0)
+    natural_col = jnp.zeros((1, total), jnp.int32)
+    natural_row = jnp.zeros((blocks, 1), jnp.int32)
     for b in range(blocks):
-        natural_col = jnp.where(lane_block == b, order_ref[b], natural_col)
-        natural_row = jnp.where(row_block == b, order_ref[b], natural_row)
+        natural = order_ref[:, b : b + 1]
+        natural_col = jnp.where(lane_block == b, natural, natural_col)
+        natural_row = jnp.where(row_block == b, natural, natural_row)
     offset = natural_col - natural_row
     offset = jnp.where(offset < 0, offset + blocks, offset)
     hit = jnp.zeros((blocks, total), jnp.bool_)
     for k in range(pattern_ref.shape[1]):
-        hit = hit | (offset == pattern_ref[0, k])
+        hit = hit | (offset == pattern_ref[0:1, k : k + 1])
     hits[...] = hit.astype(jnp.float32)
 
-    def position(device):
-        away = me ^ device
-        half_n = rows_n // 2
-        links = (ranks // 2).bit_length() - 1
+
+def work_kernel(sizes, held, pattern_ref, order_ref, out_ref, hits, xh, xl, zh, zl, ch, cl):
+    rows_n, ranks, reps_n = sizes
+    side = held.shape[-1]
+    wide = 2 * side
+    total = xh.shape[0]
+    bigs = total // wide
+    blocks = hits.shape[0]
+    block = total // blocks
+    big_row, core, big_col = place(reps_n)
+    links = (ranks // 2).bit_length() - 1
+
+    rank = big_row * 2 + core
+
+    def chunk(a, core_of, b, rows):
+        away = rank ^ (a * 2 + core_of)
         swapped = away & 1
         order = core ^ swapped
-        spot = (away // ranks) % half_n
+        spot = (big_col ^ b) * ranks + (swapped << links)
         for step in range(links):
             bit = jnp.where(order == 0, (away >> (1 + step)) & 1, (away >> (links - step)) & 1)
-            spot = spot + bit * (half_n << step)
-        return away // ranks >= half_n, spot + swapped * (half_n << links)
-
-    def chunk(device, rows):
-        far, spot = position(device)
-        return jnp.where(far, far_ref[spot, rows, :], near_ref[spot, rows, :])
+            spot = spot + (bit << step)
+        return held[spot, rows, :]
 
     def put(h, l, value, r, c):
         high, low = split(value)
@@ -149,22 +150,22 @@
     def span(index, width):
         return slice(index * width, (index + 1) * width)
 
-    for a in range(bigs):
-        for b in range(bigs):
-            if a == b:
-                continue
+    def at(index, width):
+        return pl.ds(pl.multiple_of(index * width, width), width)
+
+    def unpack(a, b):
+        if a != b:
             for j in range(2):
                 k = j if a < b else 1 - j
-                value = chunk(b * ranks + a * 2 + j, slice(0, side))
+                value = chunk(a, j, b, slice(0, side))
                 r, c = span(2 * a + j, side), span(2 * b + k, side)
                 put(xh, xl, value, r, c)
                 put(xh, xl, value.T, c, r)
-    i, j = iotas(side)
-    for a in range(bigs):
-        first = a * ranks + a * 2
-        m0 = chunk(first, slice(0, side))
-        m1 = chunk(first + 1, slice(0, side))
-        diagonal = chunk(first, slice(side, side + 1))
+            return
+        i, j = iotas(side)
+        m0 = chunk(a, 0, a, slice(0, side))
+        m1 = chunk(a, 1, a, slice(0, side))
+        diagonal = chunk(a, 0, a, slice(side, side + 1))
         t0, t1 = m0.T, m1.T
         r0, r1 = span(2 * a, side), span(2 * a + 1, side)
         put(xh, xl, jnp.where(i >= j, m0, t0), r0, r0)
@@ -178,36 +179,44 @@
             parts.append(value[span(b, block)] * hits[pl.ds(first_block + b, 1), cols])
         return jnp.concatenate(parts, axis=0)
 
+    def mirrored(h, l, value, a, b):
+        put(h, l, value, span(a, wide), span(b, wide))
+        if a != b:
+            put(h, l, value.T, span(b, wide), span(a, wide))
+
+    write_mask(pattern_ref, order_ref, hits)
+
     for b in reversed(range(bigs)):
-        r, c = slice(0, (b + 1) * wide), span(b, wide)
-        square = product(xh[r, :], xl[r, :], xh[:, c], xl[:, c])
-        value = 3.0 * (xh[r, c].astype(jnp.float32) + xl[r, c].astype(jnp.float32)) - 2.0 * square
-        put(zh, zl, value, r, c)
-        if b:
-            up = slice(0, b * wide)
-            put(zh, zl, value[up].T, c, up)
-    cols = pl.ds(pl.multiple_of(big_col * wide, wide), wide)
-    rank = big_row * 2 + core
-    rows = pl.ds(pl.multiple_of(rank * side, side), side)
-    late = slice(wide, total)
+        for a in reversed(range(b + 1)):
+            r, c = span(a, wide), span(b, wide)
+            if b == bigs - 1:
+                for k in range(a, -1, -1):
+                    unpack(a, k)
+                    if a != k:
+                        unpack(k, a)
+            square = product(xh[r, :], xl[r, :], xh[:, c], xl[:, c])
+            value = 3.0 * (xh[r, c].astype(jnp.float32) + xl[r, c].astype(jnp.float32)) - 2.0 * square
+            mirrored(zh, zl, value, a, b)
+
+    cols = at(big_col, wide)
+    rows = at(rank, side)
+
+    def term(k):
+        r = span(k, wide)
+        return product(ch[rows, r], cl[rows, r], ch[r, :], cl[r, :])
+
+    square = None
     for b in reversed(range(bigs)):
-        if b == 0:
-            partial = product(ch[:, late], cl[:, late], ch[late, cols], cl[late, cols])
-        r, c = slice(0, (b + 1) * wide), span(b, wide)
-        value = masked(product(xh[r, :], xl[r, :], zh[:, c], zl[:, c]), 0, c)
-        put(ch, cl, value, r, c)
-        if b:
-            up = slice(0, b * wide)
-            put(ch, cl, value[up].T, c, up)
-
-    first = slice(0, wide)
-    result = jnp.zeros((side, wide), jnp.float32)
-    for b in range(bigs):
-        r = span(b, wide)
-        square = partial[r] + product(ch[r, first], cl[r, first], ch[first, cols], cl[first, cols])
-        value = 3.0 * (ch[r, cols].astype(jnp.float32) + cl[r, cols].astype(jnp.float32)) - 2.0 * square
-        vh, vl = split(value)
-        result = result + product(ch[rows, r], cl[rows, r], vh, vl)
+        for a in reversed(range(b + 1)):
+            r, c = span(a, wide), span(b, wide)
+            value = product(xh[r, :], xl[r, :], zh[:, c], zl[:, c])
+            if a == 0 and b + 1 < bigs:
+                square = term(b + 1) if square is None else square + term(b + 1)
+            mirrored(ch, cl, masked(value, a * (wide // block), c), a, b)
+    square = square + term(0)
+    value = 3.0 * (ch[rows, :].astype(jnp.float32) + cl[rows, :].astype(jnp.float32)) - 2.0 * square
+    vh, vl = split(value)
+    result = product(vh, vl, ch[:, cols], cl[:, cols])
     out_ref[...] = masked(result, rank * (side // block), cols)
 
 
@@ -225,7 +234,6 @@
                 pairs.append((z * ranks + rank, z2 * ranks + rank2))
         return lax.ppermute(value, AXES, pairs)
 
-    smem = pl.BlockSpec(memory_space=pltpu.SMEM)
     vmem = pl.BlockSpec(memory_space=pltpu.VMEM)
     mine = pl.pallas_call(
         functools.partial(pack_kernel, reps_n),
@@ -235,29 +243,25 @@
         compiler_params=pltpu.CompilerParams(vmem_limit_bytes=PACK_BYTES),
         name="pack",
     )(density)
-    parts = [mine[None]]
-    for away in range(1, rows_n):
-        parts.append(swap(mine, lambda z, r, away=away: (z ^ away, r))[None])
     links = (ranks // 2).bit_length() - 1
     held = []
-    for half in (parts[: rows_n // 2], parts[rows_n // 2 :]):
-        value = jnp.concatenate(half, axis=0)
+    for away in range(rows_n):
+        value = (swap(mine, lambda z, r: (z ^ away, r)) if away else mine)[None]
         for step in range(links):
             bits = (2 << step, 1 << (links - step))
             value = jnp.concatenate([value, swap(value, lambda z, r: (z, r ^ bits[r % 2]))], axis=0)
-        held.append(jnp.concatenate([value, swap(value, lambda z, r: (z, r ^ 1))], axis=0))
-
-    blocks = grid_order.shape[0]
-    bf16 = pltpu.VMEM((total, total), jnp.bfloat16)
+        held += [value, swap(value, lambda z, r: (z, r ^ 1))]
+
     return pl.pallas_call(
         functools.partial(work_kernel, (rows_n, ranks, reps_n)),
         out_shape=jax.ShapeDtypeStruct((side, wide), jnp.float32),
-        in_specs=[smem, smem, vmem, vmem],
+        in_specs=[vmem] * 3,
         out_specs=vmem,
-        scratch_shapes=[pltpu.VMEM((blocks, total), jnp.float32)] + [bf16] * 6,
+        scratch_shapes=[pltpu.VMEM((grid_order.shape[0], total), jnp.float32)]
+        + [pltpu.VMEM((total, total), jnp.bfloat16)] * 6,
         compiler_params=pltpu.CompilerParams(vmem_limit_bytes=WORK_BYTES),
         name="purify",
-    )(pattern, grid_order, *held)
+    )(jnp.concatenate(held, axis=0), pattern, grid_order[None])
 
 
 def fits(shape, side, wide, total):

time: 43.1 us -> 38.8 us (0.900)
  waiting for transfers between devices: 15.7 us -> 11.8 us
  Pallas kernels: 14.7 us -> 11.1 us
  starting transfers between devices: 11.2 us -> 14.3 us
    ppermute x9 -> x15, waiting for transfers between devices: 15.7 us -> 11.8 us  [swap(): return lax.ppermute(value, AXES, pairs)]
    pallas_call x1, Pallas kernels: 14.7 us -> 11.1 us  [whole(): pl.pallas_call(functools.partial(work_kernel, (rows_n, ranks, reps_n)), o...]
    ppermute x9 -> x15, starting transfers between devices: 11.2 us -> 14.3 us  [swap(): return lax.ppermute(value, AXES, pairs)]
    unnamed x14 -> x21, local copies, waits for them, and re-layouts: 1.01 us -> 1.08 us
  transfers between devices with their start and end apart: 9 -> 15, of which waited for: 7 -> 8; matrix products, arithmetic and copies ran while one was open for 1% -> 1% of each run, Pallas kernels for 0% -> 0%
where the time goes in v3:
time: 38.8 us; the launch traced here: 38.6 us
  starting transfers between devices  14.3 us (37%)
  waiting for transfers between devices  11.8 us (30%)
  Pallas kernels  11.1 us (29%)
  local copies, waits for them, and re-layouts  1.1 us (3%)
    ppermute x15, starting transfers between devices, swap(): return lax.ppermute(value, AXES, pairs)  14.3 us
    ppermute x15, waiting for transfers between devices, swap(): return lax.ppermute(value, AXES, pairs)  11.8 us
    pallas_call x1, Pallas kernels, whole(): pl.pallas_call(functools.partial(work_kernel, (rows_n, ranks, reps_n)), o...  11.1 us
    unnamed x21, local copies, waits for them, and re-layouts  1.08 us
  transfers between devices with their start and end apart: 15, of which 8 were waited for; matrix products, arithmetic and copies ran while one was open for 1% of the time, Pallas kernels for 0%

profile of v3, /device:TPU:0, one launch (start us, length us, event | category | flops | bytes accessed | tf_op | source)
XLA Modules:
  0.0 38.6 jit_solution(7814222867472036225)
XLA Ops:
  0.0 0.0 copy-start
  0.0 0.9 %copy-done = f32[128,256]{1,0:T(8,128)S(1)} copy-done((f32[128,256]{1,0:T(8,128)S(1)}, f32[128,256]{1,0:T(8,128)}, u32[]{:S(2)}) %copy-start) | copy-done | bytes 131096
  0.9 3.0 %collective-permute-start.3 = (f32[136,128]{1,0:T(8,128)S(1)}, f32[136,128]{1,0:T(8,128)S(1)}, u32[]{:S(2)}, u32[]{:S(2)}) collective-permute-start(f32[136,128]{1,0:T(8,128)S(1)} %pack.1), channel_id=1, source_target_pairs={{0,8},{1,9},{2,10},{3,11},{4,12},{5,13},{6,14},{7,15},{8,0},{9,1},... | collective-permute-start | bytes 208904 | tf_op jit(solution)/shard_map/ppermute | solution.py:235
  3.9 2.6 %collective-permute-start.7 = (f32[136,128]{1,0:T(8,128)S(1)}, f32[136,128]{1,0:T(8,128)S(1)}, u32[]{:S(2)}, u32[]{:S(2)}) collective-permute-start(f32[136,128]{1,0:T(8,128)S(1)} %pack.1), channel_id=1, source_target_pairs={{0,16},{1,17},{2,18},{3,19},{4,20},{5,21},{6,22},{7,23},{8,24},{9,... | collective-permute-start | bytes 208904 | tf_op jit(solution)/shard_map/ppermute | solution.py:235
  6.5 0.0 collective-permute-start.11
  6.5 1.7 %collective-permute-start = (f32[1,136,128]{2,1,0:T(8,128)S(1)}, f32[1,136,128]{2,1,0:T(8,128)S(1)}, u32[]{:S(2)}, u32[]{:S(2)}) collective-permute-start(f32[1,136,128]{2,1,0:T(8,128)S(1)} %bitcast.9), channel_id=1, source_target_pairs={{0,2},{1,5},{2,0},{3,7},{4,6},{5,1},{6,4},{7,3},{8,10},{9,13},{10,... | collective-permute-start | bytes 208904 | tf_op jit(solution)/shard_map/ppermute | solution.py:235
  8.3 2.6 %collective-permute-done = f32[1,136,128]{2,1,0:T(8,128)S(1)} collective-permute-done((f32[1,136,128]{2,1,0:T(8,128)S(1)}, f32[1,136,128]{2,1,0:T(8,128)S(1)}, u32[]{:S(2)}, u32[]{:S(2)}) %collective-permute-start) | collective-permute-done | bytes 69664 | tf_op jit(solution)/shard_map/ppermute | solution.py:235
  10.9 1.8 %collective-permute-start.1 = (f32[2,136,128]{2,1,0:T(8,128)S(1)}, f32[2,136,128]{2,1,0:T(8,128)S(1)}, u32[]{:S(2)}, u32[]{:S(2)}) collective-permute-start(f32[2,136,128]{2,1,0:T(8,128)S(1)} %pad_maximum_fusion.4), channel_id=1, source_target_pairs={{0,4},{1,3},{2,6},{3,1},{4,0},{5,7},{6,2},{7,5},{8,12},{9,11},{10,... | collective-permute-start | bytes 417800 | tf_op jit(solution)/shard_map/ppermute | solution.py:235
  12.6 0.0 collective-permute-done.3
  12.6 1.5 %collective-permute-start.4 = (f32[1,136,128]{2,1,0:T(8,128)S(1)}, f32[1,136,128]{2,1,0:T(8,128)S(1)}, u32[]{:S(2)}, u32[]{:S(2)}) collective-permute-start(f32[1,136,128]{2,1,0:T(8,128)S(1)} %bitcast.19), channel_id=1, source_target_pairs={{0,2},{1,5},{2,0},{3,7},{4,6},{5,1},{6,4},{7,3},{8,10},{9,13},{10,... | collective-permute-start | bytes 208904 | tf_op jit(solution)/shard_map/ppermute | solution.py:235
  14.2 0.0 collective-permute-done.7
  14.2 0.5 %collective-permute-start.8 = (f32[1,136,128]{2,1,0:T(8,128)S(1)}, f32[1,136,128]{2,1,0:T(8,128)S(1)}, u32[]{:S(2)}, u32[]{:S(2)}) collective-permute-start(f32[1,136,128]{2,1,0:T(8,128)S(1)} %bitcast.16), channel_id=1, source_target_pairs={{0,2},{1,5},{2,0},{3,7},{4,6},{5,1},{6,4},{7,3},{8,10},{9,13},{10,... | collective-permute-start | bytes 208904 | tf_op jit(solution)/shard_map/ppermute | solution.py:235
  14.7 0.0 collective-permute-done.11
  14.7 1.5 %collective-permute-start.12 = (f32[1,136,128]{2,1,0:T(8,128)S(1)}, f32[1,136,128]{2,1,0:T(8,128)S(1)}, u32[]{:S(2)}, u32[]{:S(2)}) collective-permute-start(f32[1,136,128]{2,1,0:T(8,128)S(1)} %bitcast.13), channel_id=1, source_target_pairs={{0,2},{1,5},{2,0},{3,7},{4,6},{5,1},{6,4},{7,3},{8,10},{9,13},{10,... | collective-permute-start | bytes 208904 | tf_op jit(solution)/shard_map/ppermute | solution.py:235
  16.2 1.3 %collective-permute-done.4 = f32[1,136,128]{2,1,0:T(8,128)S(1)} collective-permute-done((f32[1,136,128]{2,1,0:T(8,128)S(1)}, f32[1,136,128]{2,1,0:T(8,128)S(1)}, u32[]{:S(2)}, u32[]{:S(2)}) %collective-permute-start.4) | collective-permute-done | bytes 69664 | tf_op jit(solution)/shard_map/ppermute | solution.py:235
  17.5 0.1 collective-permute-start.5
  17.6 1.7 %collective-permute-done.8 = f32[1,136,128]{2,1,0:T(8,128)S(1)} collective-permute-done((f32[1,136,128]{2,1,0:T(8,128)S(1)}, f32[1,136,128]{2,1,0:T(8,128)S(1)}, u32[]{:S(2)}, u32[]{:S(2)}) %collective-permute-start.8) | collective-permute-done | bytes 69664 | tf_op jit(solution)/shard_map/ppermute | solution.py:235
  19.3 0.6 %collective-permute-start.9 = (f32[2,136,128]{2,1,0:T(8,128)S(1)}, f32[2,136,128]{2,1,0:T(8,128)S(1)}, u32[]{:S(2)}, u32[]{:S(2)}) collective-permute-start(f32[2,136,128]{2,1,0:T(8,128)S(1)} %pad_maximum_fusion.6), channel_id=1, source_target_pairs={{0,4},{1,3},{2,6},{3,1},{4,0},{5,7},{6,2},{7,5},{8,12},{9,11},{10,... | collective-permute-start | bytes 417800 | tf_op jit(solution)/shard_map/ppermute | solution.py:235
  19.8 0.9 %collective-permute-done.12 = f32[1,136,128]{2,1,0:T(8,128)S(1)} collective-permute-done((f32[1,136,128]{2,1,0:T(8,128)S(1)}, f32[1,136,128]{2,1,0:T(8,128)S(1)}, u32[]{:S(2)}, u32[]{:S(2)}) %collective-permute-start.12) | collective-permute-done | bytes 69664 | tf_op jit(solution)/shard_map/ppermute | solution.py:235
  20.8 0.7 %collective-permute-start.13 = (f32[2,136,128]{2,1,0:T(8,128)S(1)}, f32[2,136,128]{2,1,0:T(8,128)S(1)}, u32[]{:S(2)}, u32[]{:S(2)}) collective-permute-start(f32[2,136,128]{2,1,0:T(8,128)S(1)} %pad_maximum_fusion.7), channel_id=1, source_target_pairs={{0,4},{1,3},{2,6},{3,1},{4,0},{5,7},{6,2},{7,5},{8,12},{9,11},{10,... | collective-permute-start | bytes 417800 | tf_op jit(solution)/shard_map/ppermute | solution.py:235
  21.4 0.0 collective-permute-done.1
  21.5 0.1 collective-permute-start.2
  21.6 1.0 %collective-permute-done.5 = f32[2,136,128]{2,1,0:T(8,128)S(1)} collective-permute-done((f32[2,136,128]{2,1,0:T(8,128)S(1)}, f32[2,136,128]{2,1,0:T(8,128)S(1)}, u32[]{:S(2)}, u32[]{:S(2)}) %collective-permute-start.5) | collective-permute-done | bytes 139296 | tf_op jit(solution)/shard_map/ppermute | solution.py:235
  22.6 0.1 collective-permute-start.6
  22.7 1.7 %collective-permute-done.9 = f32[2,136,128]{2,1,0:T(8,128)S(1)} collective-permute-done((f32[2,136,128]{2,1,0:T(8,128)S(1)}, f32[2,136,128]{2,1,0:T(8,128)S(1)}, u32[]{:S(2)}, u32[]{:S(2)}) %collective-permute-start.9) | collective-permute-done | bytes 139296 | tf_op jit(solution)/shard_map/ppermute | solution.py:235
  24.4 0.0 copy-start.1
  24.4 0.0 copy-start.2
  24.4 0.1 collective-permute-start.10
  24.5 1.4 %collective-permute-done.13 = f32[2,136,128]{2,1,0:T(8,128)S(1)} collective-permute-done((f32[2,136,128]{2,1,0:T(8,128)S(1)}, f32[2,136,128]{2,1,0:T(8,128)S(1)}, u32[]{:S(2)}, u32[]{:S(2)}) %collective-permute-start.13) | collective-permute-done | bytes 139296 | tf_op jit(solution)/shard_map/ppermute | solution.py:235
  25.9 0.1 collective-permute-start.14
  26.0 0.0 collective-permute-done.2
  26.1 0.0 collective-permute-done.6
  26.2 0.0 collective-permute-done.10
  26.2 1.3 %collective-permute-done.14 = f32[4,136,128]{2,1,0:T(8,128)S(1)} collective-permute-done((f32[4,136,128]{2,1,0:T(8,128)S(1)}, f32[4,136,128]{2,1,0:T(8,128)S(1)}, u32[]{:S(2)}, u32[]{:S(2)}) %collective-permute-start.14) | collective-permute-done | bytes 278560 | tf_op jit(solution)/shard_map/ppermute | solution.py:235
  27.5 0.0 copy-done.1
  27.6 0.0 copy-done.2
  27.6 11.1 %purify.1 = f32[128,256]{1,0:T(8,128)} custom-call(f32[32,136,128]{2,1,0:T(8,128)S(1)} %constant_dynamic-update-slice_fusion.held, s32[16,9]{1,0:T(8,128)S(1)} %copy-done.1, s32[1,16]{1,0:T(1,128)S(1)} %bitcast.12), custom_call_target="tpu_custom_call" | custom-call | tf_op jit(solution)/shard_map/purify/pallas_call | solution.py:255
  (25 shorter events, 0.3 us)
Async XLA Ops:
  0.0 0.9 %copy-start = (f32[128,256]{1,0:T(8,128)S(1)}, f32[128,256]{1,0:T(8,128)}, u32[]{:S(2)}) copy-start(f32[128,256]{1,0:T(8,128)} %x_ref.1) | copy-start | bytes 393220
  0.9 11.7 %collective-permute-start.3 = (f32[136,128]{1,0:T(8,128)S(1)}, f32[136,128]{1,0:T(8,128)S(1)}, u32[]{:S(2)}, u32[]{:S(2)}) collective-permute-start(f32[136,128]{1,0:T(8,128)S(1)} %pack.1), channel_id=1, source_target_pairs={{0,8},{1,9},{2,10},{3,11},{4,12},{5,13},{6,14},{7,15},{8,0},{9,1},... | collective-permute-start | bytes 208904 | tf_op jit(solution)/shard_map/ppermute | solution.py:235
  3.9 10.2 %collective-permute-start.7 = (f32[136,128]{1,0:T(8,128)S(1)}, f32[136,128]{1,0:T(8,128)S(1)}, u32[]{:S(2)}, u32[]{:S(2)}) collective-permute-start(f32[136,128]{1,0:T(8,128)S(1)} %pack.1), channel_id=1, source_target_pairs={{0,16},{1,17},{2,18},{3,19},{4,20},{5,21},{6,22},{7,23},{8,24},{9,... | collective-permute-start | bytes 208904 | tf_op jit(solution)/shard_map/ppermute | solution.py:235
  6.5 8.1 %collective-permute-start.11 = (f32[136,128]{1,0:T(8,128)S(1)}, f32[136,128]{1,0:T(8,128)S(1)}, u32[]{:S(2)}, u32[]{:S(2)}) collective-permute-start(f32[136,128]{1,0:T(8,128)S(1)} %pack.1), channel_id=1, source_target_pairs={{0,24},{1,25},{2,26},{3,27},{4,28},{5,29},{6,30},{7,31},{8,16},{9,... | collective-permute-start | bytes 208904 | tf_op jit(solution)/shard_map/ppermute | solution.py:235
  6.5 4.3 %collective-permute-start = (f32[1,136,128]{2,1,0:T(8,128)S(1)}, f32[1,136,128]{2,1,0:T(8,128)S(1)}, u32[]{:S(2)}, u32[]{:S(2)}) collective-permute-start(f32[1,136,128]{2,1,0:T(8,128)S(1)} %bitcast.9), channel_id=1, source_target_pairs={{0,2},{1,5},{2,0},{3,7},{4,6},{5,1},{6,4},{7,3},{8,10},{9,13},{10,... | collective-permute-start | bytes 208904 | tf_op jit(solution)/shard_map/ppermute | solution.py:235
  10.9 10.6 %collective-permute-start.1 = (f32[2,136,128]{2,1,0:T(8,128)S(1)}, f32[2,136,128]{2,1,0:T(8,128)S(1)}, u32[]{:S(2)}, u32[]{:S(2)}) collective-permute-start(f32[2,136,128]{2,1,0:T(8,128)S(1)} %pad_maximum_fusion.4), channel_id=1, source_target_pairs={{0,4},{1,3},{2,6},{3,1},{4,0},{5,7},{6,2},{7,5},{8,12},{9,11},{10,... | collective-permute-start | bytes 417800 | tf_op jit(solution)/shard_map/ppermute | solution.py:235
  12.6 4.8 %collective-permute-start.4 = (f32[1,136,128]{2,1,0:T(8,128)S(1)}, f32[1,136,128]{2,1,0:T(8,128)S(1)}, u32[]{:S(2)}, u32[]{:S(2)}) collective-permute-start(f32[1,136,128]{2,1,0:T(8,128)S(1)} %bitcast.19), channel_id=1, source_target_pairs={{0,2},{1,5},{2,0},{3,7},{4,6},{5,1},{6,4},{7,3},{8,10},{9,13},{10,... | collective-permute-start | bytes 208904 | tf_op jit(solution)/shard_map/ppermute | solution.py:235
  14.2 5.1 %collective-permute-start.8 = (f32[1,136,128]{2,1,0:T(8,128)S(1)}, f32[1,136,128]{2,1,0:T(8,128)S(1)}, u32[]{:S(2)}, u32[]{:S(2)}) collective-permute-start(f32[1,136,128]{2,1,0:T(8,128)S(1)} %bitcast.16), channel_id=1, source_target_pairs={{0,2},{1,5},{2,0},{3,7},{4,6},{5,1},{6,4},{7,3},{8,10},{9,13},{10,... | collective-permute-start | bytes 208904 | tf_op jit(solution)/shard_map/ppermute | solution.py:235
  14.7 6.1 %collective-permute-start.12 = (f32[1,136,128]{2,1,0:T(8,128)S(1)}, f32[1,136,128]{2,1,0:T(8,128)S(1)}, u32[]{:S(2)}, u32[]{:S(2)}) collective-permute-start(f32[1,136,128]{2,1,0:T(8,128)S(1)} %bitcast.13), channel_id=1, source_target_pairs={{0,2},{1,5},{2,0},{3,7},{4,6},{5,1},{6,4},{7,3},{8,10},{9,13},{10,... | collective-permute-start | bytes 208904 | tf_op jit(solution)/shard_map/ppermute | solution.py:235
  17.5 5.1 %collective-permute-start.5 = (f32[2,136,128]{2,1,0:T(8,128)S(1)}, f32[2,136,128]{2,1,0:T(8,128)S(1)}, u32[]{:S(2)}, u32[]{:S(2)}) collective-permute-start(f32[2,136,128]{2,1,0:T(8,128)S(1)} %pad_maximum_fusion.5), channel_id=1, source_target_pairs={{0,4},{1,3},{2,6},{3,1},{4,0},{5,7},{6,2},{7,5},{8,12},{9,11},{10,... | collective-permute-start | bytes 417800 | tf_op jit(solution)/shard_map/ppermute | solution.py:235
  19.3 5.1 %collective-permute-start.9 = (f32[2,136,128]{2,1,0:T(8,128)S(1)}, f32[2,136,128]{2,1,0:T(8,128)S(1)}, u32[]{:S(2)}, u32[]{:S(2)}) collective-permute-start(f32[2,136,128]{2,1,0:T(8,128)S(1)} %pad_maximum_fusion.6), channel_id=1, source_target_pairs={{0,4},{1,3},{2,6},{3,1},{4,0},{5,7},{6,2},{7,5},{8,12},{9,11},{10,... | collective-permute-start | bytes 417800 | tf_op jit(solution)/shard_map/ppermute | solution.py:235
  20.8 5.1 %collective-permute-start.13 = (f32[2,136,128]{2,1,0:T(8,128)S(1)}, f32[2,136,128]{2,1,0:T(8,128)S(1)}, u32[]{:S(2)}, u32[]{:S(2)}) collective-permute-start(f32[2,136,128]{2,1,0:T(8,128)S(1)} %pad_maximum_fusion.7), channel_id=1, source_target_pairs={{0,4},{1,3},{2,6},{3,1},{4,0},{5,7},{6,2},{7,5},{8,12},{9,11},{10,... | collective-permute-start | bytes 417800 | tf_op jit(solution)/shard_map/ppermute | solution.py:235
  21.5 4.5 %collective-permute-start.2 = (f32[4,136,128]{2,1,0:T(8,128)S(1)}, f32[4,136,128]{2,1,0:T(8,128)S(1)}, u32[]{:S(2)}, u32[]{:S(2)}) collective-permute-start(f32[4,136,128]{2,1,0:T(8,128)S(1)} %pad_maximum_fusion), channel_id=1, source_target_pairs={{0,1},{1,0},{2,3},{3,2},{4,5},{5,4},{6,7},{7,6},{8,9},{9,8},{10,11... | collective-permute-start | bytes 835592 | tf_op jit(solution)/shard_map/ppermute | solution.py:235
  22.6 3.4 %collective-permute-start.6 = (f32[4,136,128]{2,1,0:T(8,128)S(1)}, f32[4,136,128]{2,1,0:T(8,128)S(1)}, u32[]{:S(2)}, u32[]{:S(2)}) collective-permute-start(f32[4,136,128]{2,1,0:T(8,128)S(1)} %pad_maximum_fusion.1), channel_id=1, source_target_pairs={{0,1},{1,0},{2,3},{3,2},{4,5},{5,4},{6,7},{7,6},{8,9},{9,8},{10,11... | collective-permute-start | bytes 835592 | tf_op jit(solution)/shard_map/ppermute | solution.py:235
  24.4 3.1 %copy-start.1 = (s32[16,9]{1,0:T(8,128)S(1)}, s32[16,9]{1,0:T(8,128)}, u32[]{:S(2)}) copy-start(s32[16,9]{1,0:T(8,128)} %pattern_ref.1) | copy-start | bytes 1732
  24.4 3.1 %copy-start.2 = (s32[16]{0:T(128)S(1)}, s32[16]{0:T(128)}, u32[]{:S(2)}) copy-start(s32[16]{0:T(128)} %param.5) | copy-start | bytes 196
  24.4 1.7 %collective-permute-start.10 = (f32[4,136,128]{2,1,0:T(8,128)S(1)}, f32[4,136,128]{2,1,0:T(8,128)S(1)}, u32[]{:S(2)}, u32[]{:S(2)}) collective-permute-start(f32[4,136,128]{2,1,0:T(8,128)S(1)} %pad_maximum_fusion.2), channel_id=1, source_target_pairs={{0,1},{1,0},{2,3},{3,2},{4,5},{5,4},{6,7},{7,6},{8,9},{9,8},{10,11... | collective-permute-start | bytes 835592 | tf_op jit(solution)/shard_map/ppermute | solution.py:235
  25.9 1.6 %collective-permute-start.14 = (f32[4,136,128]{2,1,0:T(8,128)S(1)}, f32[4,136,128]{2,1,0:T(8,128)S(1)}, u32[]{:S(2)}, u32[]{:S(2)}) collective-permute-start(f32[4,136,128]{2,1,0:T(8,128)S(1)} %pad_maximum_fusion.3), channel_id=1, source_target_pairs={{0,1},{1,0},{2,3},{3,2},{4,5},{5,4},{6,7},{7,6},{8,9},{9,8},{10,11... | collective-permute-start | bytes 835592 | tf_op jit(solution)/shard_map/ppermute | solution.py:235

commit v4 on v3

--- a/solution.py
+++ b/solution.py
@@ -11,6 +11,7 @@
 AXES = ("row", "col", "rep")
 PACK_BYTES = 2 * 2**20
 WORK_BYTES = 28 * 2**20
+FLIPPED = 0b0011
 EXTRA = 8
 
 
@@ -135,8 +136,9 @@
     def chunk(a, core_of, b, rows):
         away = rank ^ (a * 2 + core_of)
         swapped = away & 1
-        order = core ^ swapped
-        spot = (big_col ^ b) * ranks + (swapped << links)
+        chain = big_col ^ b
+        order = core ^ swapped ^ ((FLIPPED >> chain) & 1)
+        spot = chain * ranks + (swapped << links)
         for step in range(links):
             bit = jnp.where(order == 0, (away >> (1 + step)) & 1, (away >> (links - step)) & 1)
             spot = spot + (bit << step)
@@ -194,7 +196,15 @@
                     unpack(a, k)
                     if a != k:
                         unpack(k, a)
-            square = product(xh[r, :], xl[r, :], xh[:, c], xl[:, c])
+            if a == b:
+                both = jnp.dot(
+                    xh[r, :],
+                    jnp.concatenate([xh[:, c], xl[:, c]], axis=1),
+                    preferred_element_type=jnp.float32,
+                )
+                square = both[:, :wide] + (both[:, wide:] + both[:, wide:].T)
+            else:
+                square = product(xh[r, :], xl[r, :], xh[:, c], xl[:, c])
             value = 3.0 * (xh[r, c].astype(jnp.float32) + xl[r, c].astype(jnp.float32)) - 2.0 * square
             mirrored(zh, zl, value, a, b)
 
@@ -244,13 +254,22 @@
         name="pack",
     )(density)
     links = (ranks // 2).bit_length() - 1
+    chains = [*range(1, rows_n, 2), *range(rows_n - 2, 0, -2)]
+    value, last = [mine[None]] * rows_n, None
+    for z_away in chains:
+        value[z_away] = swap(mine, lambda z, r: (z ^ z_away, r))[None]
+    for step in range(links):
+        for chain in [*chains, 0]:
+            if step and not chain:
+                value[0], last = lax.optimization_barrier((value[0], last))
+            bits = (2 << step, 1 << (links - step))
+            flip = FLIPPED >> chain & 1
+            came = swap(value[chain], lambda z, r: (z, r ^ bits[r % 2 ^ flip]))
+            value[chain] = jnp.concatenate([value[chain], came], axis=0)
+            last = came if not step and chain == rows_n - 1 else last
     held = []
-    for away in range(rows_n):
-        value = (swap(mine, lambda z, r: (z ^ away, r)) if away else mine)[None]
-        for step in range(links):
-            bits = (2 << step, 1 << (links - step))
-            value = jnp.concatenate([value, swap(value, lambda z, r: (z, r ^ bits[r % 2]))], axis=0)
-        held += [value, swap(value, lambda z, r: (z, r ^ 1))]
+    for chain in range(rows_n):
+        held += [value[chain], swap(value[chain], lambda z, r: (z, r ^ 1))]
 
     return pl.pallas_call(
         functools.partial(work_kernel, (rows_n, ranks, reps_n)),

time: 38.8 us -> 37.1 us (0.956)
  waiting for transfers between devices: 11.8 us -> 7.08 us
  starting transfers between devices: 14.3 us -> 17.5 us
    ppermute x15, waiting for transfers between devices: 11.8 us -> 7.08 us  [swap(): return lax.ppermute(value, AXES, pairs)]
    ppermute x15, starting transfers between devices: 14.3 us -> 17.5 us  [swap(): return lax.ppermute(value, AXES, pairs)]
    unnamed x21 -> x20, local copies, waits for them, and re-layouts: 1.08 us -> 1.08 us
  transfers between devices with their start and end apart: 15 -> 15, of which waited for: 8 -> 6; matrix products, arithmetic and copies ran while one was open for 1% -> 1% of each run, Pallas kernels for 0% -> 0%
where the time goes in v4:
time: 37.1 us; the launch traced here: 37 us
  starting transfers between devices  17.5 us (47%)
  Pallas kernels  10.9 us (29%)
  waiting for transfers between devices  7.08 us (19%)
  local copies, waits for them, and re-layouts  1.1 us (3%)
    ppermute x15, starting transfers between devices, swap(): return lax.ppermute(value, AXES, pairs)  17.5 us
    pallas_call x1, Pallas kernels, whole(): pl.pallas_call(functools.partial(work_kernel, (rows_n, ranks, reps_n)), o...  10.9 us
    ppermute x15, waiting for transfers between devices, swap(): return lax.ppermute(value, AXES, pairs)  7.08 us
    unnamed x20, local copies, waits for them, and re-layouts  1.08 us
  transfers between devices with their start and end apart: 15, of which 6 were waited for; matrix products, arithmetic and copies ran while one was open for 1% of the time, Pallas kernels for 0%

profile of v4, /device:TPU:0, one launch (start us, length us, event | category | flops | bytes accessed | tf_op | source)
XLA Modules:
  0.0 37.0 jit_solution(12495459681829485831)
XLA Ops:
  0.0 0.0 copy-start
  0.0 0.9 %copy-done = f32[128,256]{1,0:T(8,128)S(1)} copy-done((f32[128,256]{1,0:T(8,128)S(1)}, f32[128,256]{1,0:T(8,128)}, u32[]{:S(2)}) %copy-start) | copy-done | bytes 131096
  0.9 5.0 %collective-permute-start.1 = (f32[136,128]{1,0:T(8,128)S(1)}, f32[136,128]{1,0:T(8,128)S(1)}, u32[]{:S(2)}, u32[]{:S(2)}) collective-permute-start(f32[136,128]{1,0:T(8,128)S(1)} %pack.1), channel_id=1, source_target_pairs={{0,24},{1,25},{2,26},{3,27},{4,28},{5,29},{6,30},{7,31},{8,16},{9,... | collective-permute-start | bytes 208904 | tf_op jit(solution)/shard_map/ppermute | solution.py:245
  6.0 0.0 collective-permute-start.5
  6.0 0.6 %collective-permute-start.9 = (f32[136,128]{1,0:T(8,128)S(1)}, f32[136,128]{1,0:T(8,128)S(1)}, u32[]{:S(2)}, u32[]{:S(2)}) collective-permute-start(f32[136,128]{1,0:T(8,128)S(1)} %pack.1), channel_id=1, source_target_pairs={{0,16},{1,17},{2,18},{3,19},{4,20},{5,21},{6,22},{7,23},{8,24},{9,... | collective-permute-start | bytes 208904 | tf_op jit(solution)/shard_map/ppermute | solution.py:245
  6.6 1.6 %collective-permute-start = (f32[1,136,128]{2,1,0:T(8,128)S(1)}, f32[1,136,128]{2,1,0:T(8,128)S(1)}, u32[]{:S(2)}, u32[]{:S(2)}) collective-permute-start(f32[1,136,128]{2,1,0:T(8,128)S(1)} %bitcast.8), channel_id=1, source_target_pairs={{0,4},{1,3},{2,6},{3,1},{4,0},{5,7},{6,2},{7,5},{8,12},{9,11},{10,... | collective-permute-start | bytes 208904 | tf_op jit(solution)/shard_map/ppermute | solution.py:245
  8.2 0.7 %collective-permute-done.1 = f32[136,128]{1,0:T(8,128)S(1)} collective-permute-done((f32[136,128]{1,0:T(8,128)S(1)}, f32[136,128]{1,0:T(8,128)S(1)}, u32[]{:S(2)}, u32[]{:S(2)}) %collective-permute-start.1) | collective-permute-done | bytes 69664 | tf_op jit(solution)/shard_map/ppermute | solution.py:245
  9.0 1.5 %collective-permute-start.2 = (f32[1,136,128]{2,1,0:T(8,128)S(1)}, f32[1,136,128]{2,1,0:T(8,128)S(1)}, u32[]{:S(2)}, u32[]{:S(2)}) collective-permute-start(f32[1,136,128]{2,1,0:T(8,128)S(1)} %bitcast.11), channel_id=1, source_target_pairs={{0,2},{1,5},{2,0},{3,7},{4,6},{5,1},{6,4},{7,3},{8,10},{9,13},{10,... | collective-permute-start | bytes 208904 | tf_op jit(solution)/shard_map/ppermute | solution.py:245
  10.5 0.3 collective-permute-done.5
  10.8 1.6 %collective-permute-start.6 = (f32[1,136,128]{2,1,0:T(8,128)S(1)}, f32[1,136,128]{2,1,0:T(8,128)S(1)}, u32[]{:S(2)}, u32[]{:S(2)}) collective-permute-start(f32[1,136,128]{2,1,0:T(8,128)S(1)} %bitcast.17), channel_id=1, source_target_pairs={{0,4},{1,3},{2,6},{3,1},{4,0},{5,7},{6,2},{7,5},{8,12},{9,11},{10,... | collective-permute-start | bytes 208904 | tf_op jit(solution)/shard_map/ppermute | solution.py:245
  12.4 0.0 collective-permute-done.9
  12.4 1.6 %collective-permute-start.10 = (f32[1,136,128]{2,1,0:T(8,128)S(1)}, f32[1,136,128]{2,1,0:T(8,128)S(1)}, u32[]{:S(2)}, u32[]{:S(2)}) collective-permute-start(f32[1,136,128]{2,1,0:T(8,128)S(1)} %bitcast.14), channel_id=1, source_target_pairs={{0,2},{1,5},{2,0},{3,7},{4,6},{5,1},{6,4},{7,3},{8,10},{9,13},{10,... | collective-permute-start | bytes 208904 | tf_op jit(solution)/shard_map/ppermute | solution.py:245
  14.0 0.0 collective-permute-done
  14.0 0.0 collective-permute-done.2
  14.0 1.0 %collective-permute-start.3 = (f32[2,136,128]{2,1,0:T(8,128)S(1)}, f32[2,136,128]{2,1,0:T(8,128)S(1)}, u32[]{:S(2)}, u32[]{:S(2)}) collective-permute-start(f32[2,136,128]{2,1,0:T(8,128)S(1)} %pad_maximum_fusion.4), channel_id=1, source_target_pairs={{0,2},{1,5},{2,0},{3,7},{4,6},{5,1},{6,4},{7,3},{8,10},{9,13},{10,... | collective-permute-start | bytes 417800 | tf_op jit(solution)/shard_map/ppermute | solution.py:245
  15.0 0.8 %collective-permute-done.6 = f32[1,136,128]{2,1,0:T(8,128)S(1)} collective-permute-done((f32[1,136,128]{2,1,0:T(8,128)S(1)}, f32[1,136,128]{2,1,0:T(8,128)S(1)}, u32[]{:S(2)}, u32[]{:S(2)}) %collective-permute-start.6) | collective-permute-done | bytes 69664 | tf_op jit(solution)/shard_map/ppermute | solution.py:245
  15.9 1.6 %collective-permute-start.7 = (f32[2,136,128]{2,1,0:T(8,128)S(1)}, f32[2,136,128]{2,1,0:T(8,128)S(1)}, u32[]{:S(2)}, u32[]{:S(2)}) collective-permute-start(f32[2,136,128]{2,1,0:T(8,128)S(1)} %pad_maximum_fusion.5), channel_id=1, source_target_pairs={{0,2},{1,5},{2,0},{3,7},{4,6},{5,1},{6,4},{7,3},{8,10},{9,13},{10,... | collective-permute-start | bytes 417800 | tf_op jit(solution)/shard_map/ppermute | solution.py:245
  17.4 0.0 collective-permute-done.10
  17.5 1.8 %collective-permute-start.11 = (f32[2,136,128]{2,1,0:T(8,128)S(1)}, f32[2,136,128]{2,1,0:T(8,128)S(1)}, u32[]{:S(2)}, u32[]{:S(2)}) collective-permute-start(f32[2,136,128]{2,1,0:T(8,128)S(1)} %pad_maximum_fusion.6), channel_id=1, source_target_pairs={{0,4},{1,3},{2,6},{3,1},{4,0},{5,7},{6,2},{7,5},{8,12},{9,11},{10,... | collective-permute-start | bytes 417800 | tf_op jit(solution)/shard_map/ppermute | solution.py:245
  19.3 0.4 collective-permute-start.13
  19.6 0.0 collective-permute-done.3
  19.7 0.1 collective-permute-start.4
  19.8 2.9 %collective-permute-done.7 = f32[2,136,128]{2,1,0:T(8,128)S(1)} collective-permute-done((f32[2,136,128]{2,1,0:T(8,128)S(1)}, f32[2,136,128]{2,1,0:T(8,128)S(1)}, u32[]{:S(2)}, u32[]{:S(2)}) %collective-permute-start.7) | collective-permute-done | bytes 139296 | tf_op jit(solution)/shard_map/ppermute | solution.py:245
  22.7 0.1 collective-permute-start.8
  22.8 0.0 collective-permute-done.11
  22.8 0.6 %collective-permute-start.12 = (f32[4,136,128]{2,1,0:T(8,128)S(1)}, f32[4,136,128]{2,1,0:T(8,128)S(1)}, u32[]{:S(2)}, u32[]{:S(2)}) collective-permute-start(f32[4,136,128]{2,1,0:T(8,128)S(1)} %pad_maximum_fusion.2), channel_id=1, source_target_pairs={{0,1},{1,0},{2,3},{3,2},{4,5},{5,4},{6,7},{7,6},{8,9},{9,8},{10,11... | collective-permute-start | bytes 835592 | tf_op jit(solution)/shard_map/ppermute | solution.py:245
  23.4 1.0 %collective-permute-done.13 = f32[2,136,128]{2,1,0:T(8,128)S(1)} collective-permute-done((f32[2,136,128]{2,1,0:T(8,128)S(1)}, f32[2,136,128]{2,1,0:T(8,128)S(1)}, u32[]{:S(2)}, u32[]{:S(2)}) %collective-permute-start.13) | collective-permute-done | bytes 139296 | tf_op jit(solution)/shard_map/ppermute | solution.py:245
  24.4 0.0 copy-start.1
  24.4 0.0 copy-start.2
  24.4 0.1 collective-permute-start.14
  24.5 0.0 collective-permute-done.4
  24.6 0.0 collective-permute-done.8
  24.7 0.0 collective-permute-done.12
  24.8 1.3 %collective-permute-done.14 = f32[4,136,128]{2,1,0:T(8,128)S(1)} collective-permute-done((f32[4,136,128]{2,1,0:T(8,128)S(1)}, f32[4,136,128]{2,1,0:T(8,128)S(1)}, u32[]{:S(2)}, u32[]{:S(2)}) %collective-permute-start.14) | collective-permute-done | bytes 278560 | tf_op jit(solution)/shard_map/ppermute | solution.py:245
  26.1 0.0 copy-done.1
  26.1 0.0 copy-done.2
  26.1 10.9 %purify.1 = f32[128,256]{1,0:T(8,128)} custom-call(f32[32,136,128]{2,1,0:T(8,128)S(1)} %constant_dynamic-update-slice_fusion.held, s32[16,9]{1,0:T(8,128)S(1)} %copy-done.1, s32[1,16]{1,0:T(1,128)S(1)} %bitcast.10), custom_call_target="tpu_custom_call" | custom-call | tf_op jit(solution)/shard_map/purify/pallas_call | solution.py:274
  (24 shorter events, 0.4 us)
Async XLA Ops:
  0.0 0.9 %copy-start = (f32[128,256]{1,0:T(8,128)S(1)}, f32[128,256]{1,0:T(8,128)}, u32[]{:S(2)}) copy-start(f32[128,256]{1,0:T(8,128)} %x_ref.1) | copy-start | bytes 393220
  0.9 8.1 %collective-permute-start.1 = (f32[136,128]{1,0:T(8,128)S(1)}, f32[136,128]{1,0:T(8,128)S(1)}, u32[]{:S(2)}, u32[]{:S(2)}) collective-permute-start(f32[136,128]{1,0:T(8,128)S(1)} %pack.1), channel_id=1, source_target_pairs={{0,24},{1,25},{2,26},{3,27},{4,28},{5,29},{6,30},{7,31},{8,16},{9,... | collective-permute-start | bytes 208904 | tf_op jit(solution)/shard_map/ppermute | solution.py:245
  6.0 4.8 %collective-permute-start.5 = (f32[136,128]{1,0:T(8,128)S(1)}, f32[136,128]{1,0:T(8,128)S(1)}, u32[]{:S(2)}, u32[]{:S(2)}) collective-permute-start(f32[136,128]{1,0:T(8,128)S(1)} %pack.1), channel_id=1, source_target_pairs={{0,8},{1,9},{2,10},{3,11},{4,12},{5,13},{6,14},{7,15},{8,0},{9,1},... | collective-permute-start | bytes 208904 | tf_op jit(solution)/shard_map/ppermute | solution.py:245
  6.0 6.5 %collective-permute-start.9 = (f32[136,128]{1,0:T(8,128)S(1)}, f32[136,128]{1,0:T(8,128)S(1)}, u32[]{:S(2)}, u32[]{:S(2)}) collective-permute-start(f32[136,128]{1,0:T(8,128)S(1)} %pack.1), channel_id=1, source_target_pairs={{0,16},{1,17},{2,18},{3,19},{4,20},{5,21},{6,22},{7,23},{8,24},{9,... | collective-permute-start | bytes 208904 | tf_op jit(solution)/shard_map/ppermute | solution.py:245
  6.6 7.4 %collective-permute-start = (f32[1,136,128]{2,1,0:T(8,128)S(1)}, f32[1,136,128]{2,1,0:T(8,128)S(1)}, u32[]{:S(2)}, u32[]{:S(2)}) collective-permute-start(f32[1,136,128]{2,1,0:T(8,128)S(1)} %bitcast.8), channel_id=1, source_target_pairs={{0,4},{1,3},{2,6},{3,1},{4,0},{5,7},{6,2},{7,5},{8,12},{9,11},{10,... | collective-permute-start | bytes 208904 | tf_op jit(solution)/shard_map/ppermute | solution.py:245
  9.0 5.0 %collective-permute-start.2 = (f32[1,136,128]{2,1,0:T(8,128)S(1)}, f32[1,136,128]{2,1,0:T(8,128)S(1)}, u32[]{:S(2)}, u32[]{:S(2)}) collective-permute-start(f32[1,136,128]{2,1,0:T(8,128)S(1)} %bitcast.11), channel_id=1, source_target_pairs={{0,2},{1,5},{2,0},{3,7},{4,6},{5,1},{6,4},{7,3},{8,10},{9,13},{10,... | collective-permute-start | bytes 208904 | tf_op jit(solution)/shard_map/ppermute | solution.py:245
  10.8 5.0 %collective-permute-start.6 = (f32[1,136,128]{2,1,0:T(8,128)S(1)}, f32[1,136,128]{2,1,0:T(8,128)S(1)}, u32[]{:S(2)}, u32[]{:S(2)}) collective-permute-start(f32[1,136,128]{2,1,0:T(8,128)S(1)} %bitcast.17), channel_id=1, source_target_pairs={{0,4},{1,3},{2,6},{3,1},{4,0},{5,7},{6,2},{7,5},{8,12},{9,11},{10,... | collective-permute-start | bytes 208904 | tf_op jit(solution)/shard_map/ppermute | solution.py:245
  12.4 5.0 %collective-permute-start.10 = (f32[1,136,128]{2,1,0:T(8,128)S(1)}, f32[1,136,128]{2,1,0:T(8,128)S(1)}, u32[]{:S(2)}, u32[]{:S(2)}) collective-permute-start(f32[1,136,128]{2,1,0:T(8,128)S(1)} %bitcast.14), channel_id=1, source_target_pairs={{0,2},{1,5},{2,0},{3,7},{4,6},{5,1},{6,4},{7,3},{8,10},{9,13},{10,... | collective-permute-start | bytes 208904 | tf_op jit(solution)/shard_map/ppermute | solution.py:245
  14.0 5.6 %collective-permute-start.3 = (f32[2,136,128]{2,1,0:T(8,128)S(1)}, f32[2,136,128]{2,1,0:T(8,128)S(1)}, u32[]{:S(2)}, u32[]{:S(2)}) collective-permute-start(f32[2,136,128]{2,1,0:T(8,128)S(1)} %pad_maximum_fusion.4), channel_id=1, source_target_pairs={{0,2},{1,5},{2,0},{3,7},{4,6},{5,1},{6,4},{7,3},{8,10},{9,13},{10,... | collective-permute-start | bytes 417800 | tf_op jit(solution)/shard_map/ppermute | solution.py:245
  15.9 6.8 %collective-permute-start.7 = (f32[2,136,128]{2,1,0:T(8,128)S(1)}, f32[2,136,128]{2,1,0:T(8,128)S(1)}, u32[]{:S(2)}, u32[]{:S(2)}) collective-permute-start(f32[2,136,128]{2,1,0:T(8,128)S(1)} %pad_maximum_fusion.5), channel_id=1, source_target_pairs={{0,2},{1,5},{2,0},{3,7},{4,6},{5,1},{6,4},{7,3},{8,10},{9,13},{10,... | collective-permute-start | bytes 417800 | tf_op jit(solution)/shard_map/ppermute | solution.py:245
  17.5 5.3 %collective-permute-start.11 = (f32[2,136,128]{2,1,0:T(8,128)S(1)}, f32[2,136,128]{2,1,0:T(8,128)S(1)}, u32[]{:S(2)}, u32[]{:S(2)}) collective-permute-start(f32[2,136,128]{2,1,0:T(8,128)S(1)} %pad_maximum_fusion.6), channel_id=1, source_target_pairs={{0,4},{1,3},{2,6},{3,1},{4,0},{5,7},{6,2},{7,5},{8,12},{9,11},{10,... | collective-permute-start | bytes 417800 | tf_op jit(solution)/shard_map/ppermute | solution.py:245
  19.3 5.1 %collective-permute-start.13 = (f32[2,136,128]{2,1,0:T(8,128)S(1)}, f32[2,136,128]{2,1,0:T(8,128)S(1)}, u32[]{:S(2)}, u32[]{:S(2)}) collective-permute-start(f32[2,136,128]{2,1,0:T(8,128)S(1)} %pad_maximum_fusion.7), channel_id=1, source_target_pairs={{0,4},{1,3},{2,6},{3,1},{4,0},{5,7},{6,2},{7,5},{8,12},{9,11},{10,... | collective-permute-start | bytes 417800 | tf_op jit(solution)/shard_map/ppermute | solution.py:245
  19.7 4.8 %collective-permute-start.4 = (f32[4,136,128]{2,1,0:T(8,128)S(1)}, f32[4,136,128]{2,1,0:T(8,128)S(1)}, u32[]{:S(2)}, u32[]{:S(2)}) collective-permute-start(f32[4,136,128]{2,1,0:T(8,128)S(1)} %pad_maximum_fusion), channel_id=1, source_target_pairs={{0,1},{1,0},{2,3},{3,2},{4,5},{5,4},{6,7},{7,6},{8,9},{9,8},{10,11... | collective-permute-start | bytes 835592 | tf_op jit(solution)/shard_map/ppermute | solution.py:245
  22.7 1.9 %collective-permute-start.8 = (f32[4,136,128]{2,1,0:T(8,128)S(1)}, f32[4,136,128]{2,1,0:T(8,128)S(1)}, u32[]{:S(2)}, u32[]{:S(2)}) collective-permute-start(f32[4,136,128]{2,1,0:T(8,128)S(1)} %pad_maximum_fusion.1), channel_id=1, source_target_pairs={{0,1},{1,0},{2,3},{3,2},{4,5},{5,4},{6,7},{7,6},{8,9},{9,8},{10,11... | collective-permute-start | bytes 835592 | tf_op jit(solution)/shard_map/ppermute | solution.py:245
  22.8 1.9 %collective-permute-start.12 = (f32[4,136,128]{2,1,0:T(8,128)S(1)}, f32[4,136,128]{2,1,0:T(8,128)S(1)}, u32[]{:S(2)}, u32[]{:S(2)}) collective-permute-start(f32[4,136,128]{2,1,0:T(8,128)S(1)} %pad_maximum_fusion.2), channel_id=1, source_target_pairs={{0,1},{1,0},{2,3},{3,2},{4,5},{5,4},{6,7},{7,6},{8,9},{9,8},{10,11... | collective-permute-start | bytes 835592 | tf_op jit(solution)/shard_map/ppermute | solution.py:245
  24.4 1.7 %copy-start.1 = (s32[16,9]{1,0:T(8,128)S(1)}, s32[16,9]{1,0:T(8,128)}, u32[]{:S(2)}) copy-start(s32[16,9]{1,0:T(8,128)} %pattern_ref.1) | copy-start | bytes 1732
  24.4 1.7 %copy-start.2 = (s32[16]{0:T(128)S(1)}, s32[16]{0:T(128)}, u32[]{:S(2)}) copy-start(s32[16]{0:T(128)} %param.5) | copy-start | bytes 196
  24.4 1.6 %collective-permute-start.14 = (f32[4,136,128]{2,1,0:T(8,128)S(1)}, f32[4,136,128]{2,1,0:T(8,128)S(1)}, u32[]{:S(2)}, u32[]{:S(2)}) collective-permute-start(f32[4,136,128]{2,1,0:T(8,128)S(1)} %pad_maximum_fusion.3), channel_id=1, source_target_pairs={{0,1},{1,0},{2,3},{3,2},{4,5},{5,4},{6,7},{7,6},{8,9},{9,8},{10,11... | collective-permute-start | bytes 835592 | tf_op jit(solution)/shard_map/ppermute | solution.py:245

commit v5 on v4

--- a/solution.py
+++ b/solution.py
@@ -11,7 +11,6 @@
 AXES = ("row", "col", "rep")
 PACK_BYTES = 2 * 2**20
 WORK_BYTES = 28 * 2**20
-FLIPPED = 0b0011
 EXTRA = 8
 
 
@@ -77,6 +76,14 @@
     )
 
 
+def chain_groups(rows_n):
+    return [group for group in ([0], [*range(1, rows_n - 1)], [rows_n - 1]) if group]
+
+
+def flipped(group):
+    return 1 - group % 2
+
+
 def place(reps_n):
     rank = lax.axis_index("col") * reps_n + lax.axis_index("rep")
     return rank // 2, rank & 1, lax.axis_index("row")
@@ -120,9 +127,12 @@
     hits[...] = hit.astype(jnp.float32)
 
 
-def work_kernel(sizes, held, pattern_ref, order_ref, out_ref, hits, xh, xl, zh, zl, ch, cl):
+def work_kernel(sizes, *refs):
     rows_n, ranks, reps_n = sizes
-    side = held.shape[-1]
+    groups = chain_groups(rows_n)
+    held, rest = refs[: len(groups)], refs[len(groups) :]
+    pattern_ref, order_ref, out_ref, hits, xh, xl, zh, zl, ch, cl = rest
+    side = held[0].shape[-1]
     wide = 2 * side
     total = xh.shape[0]
     bigs = total // wide
@@ -136,13 +146,18 @@
     def chunk(a, core_of, b, rows):
         away = rank ^ (a * 2 + core_of)
         swapped = away & 1
-        chain = big_col ^ b
-        order = core ^ swapped ^ ((FLIPPED >> chain) & 1)
-        spot = chain * ranks + (swapped << links)
-        for step in range(links):
-            bit = jnp.where(order == 0, (away >> (1 + step)) & 1, (away >> (links - step)) & 1)
-            spot = spot + (bit << step)
-        return held[spot, rows, :]
+        result = None
+        for index, group in enumerate(groups):
+            order = core ^ swapped ^ flipped(index)
+            bits = swapped << links
+            for step in range(links):
+                bit = jnp.where(order == 0, (away >> (1 + step)) & 1, (away >> (links - step)) & 1)
+                bits = bits | (bit << step)
+            chain = big_col ^ b
+            member = jnp.clip(chain - group[0], 0, len(group) - 1)
+            value = held[index][bits * len(group) + member, rows, :]
+            result = value if result is None else jnp.where(chain >= group[0], value, result)
+        return result
 
     def put(h, l, value, r, c):
         high, low = split(value)
@@ -254,33 +269,32 @@
         name="pack",
     )(density)
     links = (ranks // 2).bit_length() - 1
-    chains = [*range(1, rows_n, 2), *range(rows_n - 2, 0, -2)]
-    value, last = [mine[None]] * rows_n, None
-    for z_away in chains:
-        value[z_away] = swap(mine, lambda z, r: (z ^ z_away, r))[None]
+    came = {0: mine[None]}
+    for away in range(1, rows_n):
+        came[away] = swap(mine, lambda z, r: (z ^ away, r))[None]
+    groups = chain_groups(rows_n)
+    value = [jnp.concatenate([came[chain] for chain in group], axis=0) for group in groups]
     for step in range(links):
-        for chain in [*chains, 0]:
-            if step and not chain:
-                value[0], last = lax.optimization_barrier((value[0], last))
+        for k in reversed(range(len(groups))):
+            if step and not k:
+                value[k], _ = lax.optimization_barrier((value[k], came[rows_n // 2]))
             bits = (2 << step, 1 << (links - step))
-            flip = FLIPPED >> chain & 1
-            came = swap(value[chain], lambda z, r: (z, r ^ bits[r % 2 ^ flip]))
-            value[chain] = jnp.concatenate([value[chain], came], axis=0)
-            last = came if not step and chain == rows_n - 1 else last
+            crossed = swap(value[k], lambda z, r: (z, r ^ bits[r % 2 ^ flipped(k)]))
+            value[k] = jnp.concatenate([value[k], crossed], axis=0)
     held = []
-    for chain in range(rows_n):
-        held += [value[chain], swap(value[chain], lambda z, r: (z, r ^ 1))]
+    for one in value:
+        held.append(jnp.concatenate([one, swap(one, lambda z, r: (z, r ^ 1))], axis=0))
 
     return pl.pallas_call(
         functools.partial(work_kernel, (rows_n, ranks, reps_n)),
         out_shape=jax.ShapeDtypeStruct((side, wide), jnp.float32),
-        in_specs=[vmem] * 3,
+        in_specs=[vmem] * (len(held) + 2),
         out_specs=vmem,
         scratch_shapes=[pltpu.VMEM((grid_order.shape[0], total), jnp.float32)]
         + [pltpu.VMEM((total, total), jnp.bfloat16)] * 6,
         compiler_params=pltpu.CompilerParams(vmem_limit_bytes=WORK_BYTES),
         name="purify",
-    )(jnp.concatenate(held, axis=0), pattern, grid_order[None])
+    )(*held, pattern, grid_order[None])
 
 
 def fits(shape, side, wide, total):

time: 37.1 us -> 36.2 us (0.976)
  starting transfers between devices: 17.5 us -> 15.3 us
  waiting for transfers between devices: 7.08 us -> 8.33 us
    ppermute x15 -> x12, starting transfers between devices: 17.5 us -> 15.3 us  [swap(): return lax.ppermute(value, AXES, pairs)]
    ppermute x15 -> x12, waiting for transfers between devices: 7.08 us -> 8.33 us  [swap(): return lax.ppermute(value, AXES, pairs)]
    unnamed x20 -> x10, local copies, waits for them, and re-layouts: 1.08 us -> 0.96 us
  transfers between devices with their start and end apart: 15 -> 12, of which waited for: 6 -> 6; matrix products, arithmetic and copies ran while one was open for 1% -> 1% of each run, Pallas kernels for 0% -> 0%
where the time goes in v5:
time: 36.2 us; the launch traced here: 36.1 us
  starting transfers between devices  15.3 us (42%)
  Pallas kernels  11 us (30%)
  waiting for transfers between devices  8.33 us (23%)
  local copies, waits for them, and re-layouts  1 us (3%)
    ppermute x12, starting transfers between devices, swap(): return lax.ppermute(value, AXES, pairs)  15.3 us
    pallas_call x1, Pallas kernels, whole(): pl.pallas_call(functools.partial(work_kernel, (rows_n, ranks, reps_n)), o...  11 us
    ppermute x12, waiting for transfers between devices, swap(): return lax.ppermute(value, AXES, pairs)  8.33 us
    unnamed x10, local copies, waits for them, and re-layouts  0.96 us
  transfers between devices with their start and end apart: 12, of which 6 were waited for; matrix products, arithmetic and copies ran while one was open for 1% of the time, Pallas kernels for 0%

profile of v5, /device:TPU:0, one launch (start us, length us, event | category | flops | bytes accessed | tf_op | source)
XLA Modules:
  0.0 36.1 jit_solution(3158177691027476372)
XLA Ops:
  0.0 0.0 copy-start
  0.0 0.9 %copy-done = f32[128,256]{1,0:T(8,128)S(1)} copy-done((f32[128,256]{1,0:T(8,128)S(1)}, f32[128,256]{1,0:T(8,128)}, u32[]{:S(2)}) %copy-start) | copy-done | bytes 131096
  0.9 4.0 %collective-permute-start.1 = (f32[136,128]{1,0:T(8,128)S(1)}, f32[136,128]{1,0:T(8,128)S(1)}, u32[]{:S(2)}, u32[]{:S(2)}) collective-permute-start(f32[136,128]{1,0:T(8,128)S(1)} %pack.1), channel_id=1, source_target_pairs={{0,16},{1,17},{2,18},{3,19},{4,20},{5,21},{6,22},{7,23},{8,24},{9,... | collective-permute-start | bytes 208904 | tf_op jit(solution)/shard_map/ppermute | solution.py:260
  4.9 1.6 %collective-permute-start.4 = (f32[136,128]{1,0:T(8,128)S(1)}, f32[136,128]{1,0:T(8,128)S(1)}, u32[]{:S(2)}, u32[]{:S(2)}) collective-permute-start(f32[136,128]{1,0:T(8,128)S(1)} %pack.1), channel_id=1, source_target_pairs={{0,8},{1,9},{2,10},{3,11},{4,12},{5,13},{6,14},{7,15},{8,0},{9,1},... | collective-permute-start | bytes 208904 | tf_op jit(solution)/shard_map/ppermute | solution.py:260
  6.5 0.0 collective-permute-start.8
  6.5 1.7 %collective-permute-start = (f32[1,136,128]{2,1,0:T(8,128)S(1)}, f32[1,136,128]{2,1,0:T(8,128)S(1)}, u32[]{:S(2)}, u32[]{:S(2)}) collective-permute-start(f32[1,136,128]{2,1,0:T(8,128)S(1)} %bitcast.7), channel_id=1, source_target_pairs={{0,4},{1,3},{2,6},{3,1},{4,0},{5,7},{6,2},{7,5},{8,12},{9,11},{10,... | collective-permute-start | bytes 208904 | tf_op jit(solution)/shard_map/ppermute | solution.py:260
  8.2 0.0 collective-permute-done.1
  8.2 1.0 %collective-permute-done.4 = f32[136,128]{1,0:T(8,128)S(1)} collective-permute-done((f32[136,128]{1,0:T(8,128)S(1)}, f32[136,128]{1,0:T(8,128)S(1)}, u32[]{:S(2)}, u32[]{:S(2)}) %collective-permute-start.4) | collective-permute-done | bytes 69664 | tf_op jit(solution)/shard_map/ppermute | solution.py:260
  9.3 1.7 %collective-permute-start.5 = (f32[2,136,128]{2,1,0:T(8,128)S(1)}, f32[2,136,128]{2,1,0:T(8,128)S(1)}, u32[]{:S(2)}, u32[]{:S(2)}) collective-permute-start(f32[2,136,128]{2,1,0:T(8,128)S(1)} %pad_maximum_fusion.7), channel_id=1, source_target_pairs={{0,2},{1,5},{2,0},{3,7},{4,6},{5,1},{6,4},{7,3},{8,10},{9,13},{10,... | collective-permute-start | bytes 417800 | tf_op jit(solution)/shard_map/ppermute | solution.py:260
  10.9 1.7 %collective-permute-done.8 = f32[136,128]{1,0:T(8,128)S(1)} collective-permute-done((f32[136,128]{1,0:T(8,128)S(1)}, f32[136,128]{1,0:T(8,128)S(1)}, u32[]{:S(2)}, u32[]{:S(2)}) %collective-permute-start.8) | collective-permute-done | bytes 69664 | tf_op jit(solution)/shard_map/ppermute | solution.py:260
  12.6 1.5 %collective-permute-start.9 = (f32[1,136,128]{2,1,0:T(8,128)S(1)}, f32[1,136,128]{2,1,0:T(8,128)S(1)}, u32[]{:S(2)}, u32[]{:S(2)}) collective-permute-start(f32[1,136,128]{2,1,0:T(8,128)S(1)} %bitcast.16), channel_id=1, source_target_pairs={{0,4},{1,3},{2,6},{3,1},{4,0},{5,7},{6,2},{7,5},{8,12},{9,11},{10,... | collective-permute-start | bytes 208904 | tf_op jit(solution)/shard_map/ppermute | solution.py:260
  14.1 0.0 collective-permute-done
  14.1 1.7 %collective-permute-start.2 = (f32[2,136,128]{2,1,0:T(8,128)S(1)}, f32[2,136,128]{2,1,0:T(8,128)S(1)}, u32[]{:S(2)}, u32[]{:S(2)}) collective-permute-start(f32[2,136,128]{2,1,0:T(8,128)S(1)} %pad_maximum_fusion.6), channel_id=1, source_target_pairs={{0,2},{1,5},{2,0},{3,7},{4,6},{5,1},{6,4},{7,3},{8,10},{9,13},{10,... | collective-permute-start | bytes 417800 | tf_op jit(solution)/shard_map/ppermute | solution.py:260
  15.8 0.0 collective-permute-done.5
  15.9 1.0 %collective-permute-start.6 = (f32[4,136,128]{2,1,0:T(8,128)S(1)}, f32[4,136,128]{2,1,0:T(8,128)S(1)}, u32[]{:S(2)}, u32[]{:S(2)}) collective-permute-start(f32[4,136,128]{2,1,0:T(8,128)S(1)} %pad_maximum_fusion.4), channel_id=1, source_target_pairs={{0,4},{1,3},{2,6},{3,1},{4,0},{5,7},{6,2},{7,5},{8,12},{9,11},{10,... | collective-permute-start | bytes 835592 | tf_op jit(solution)/shard_map/ppermute | solution.py:260
  16.9 0.2 collective-permute-done.9
  17.0 1.5 %collective-permute-start.10 = (f32[2,136,128]{2,1,0:T(8,128)S(1)}, f32[2,136,128]{2,1,0:T(8,128)S(1)}, u32[]{:S(2)}, u32[]{:S(2)}) collective-permute-start(f32[2,136,128]{2,1,0:T(8,128)S(1)} %pad_maximum_fusion.8), channel_id=1, source_target_pairs={{0,2},{1,5},{2,0},{3,7},{4,6},{5,1},{6,4},{7,3},{8,10},{9,13},{10,... | collective-permute-start | bytes 417800 | tf_op jit(solution)/shard_map/ppermute | solution.py:260
  18.5 2.1 %collective-permute-done.2 = f32[2,136,128]{2,1,0:T(8,128)S(1)} collective-permute-done((f32[2,136,128]{2,1,0:T(8,128)S(1)}, f32[2,136,128]{2,1,0:T(8,128)S(1)}, u32[]{:S(2)}, u32[]{:S(2)}) %collective-permute-start.2) | collective-permute-done | bytes 139296 | tf_op jit(solution)/shard_map/ppermute | solution.py:260
  20.7 0.1 collective-permute-start.3
  20.8 1.7 %collective-permute-done.6 = f32[4,136,128]{2,1,0:T(8,128)S(1)} collective-permute-done((f32[4,136,128]{2,1,0:T(8,128)S(1)}, f32[4,136,128]{2,1,0:T(8,128)S(1)}, u32[]{:S(2)}, u32[]{:S(2)}) %collective-permute-start.6) | collective-permute-done | bytes 278560 | tf_op jit(solution)/shard_map/ppermute | solution.py:260
  22.5 0.1 pad_maximum_fusion.1
  22.5 0.1 collective-permute-start.7
  22.6 0.0 collective-permute-done.10
  22.6 0.6 %collective-permute-start.11 = (f32[4,136,128]{2,1,0:T(8,128)S(1)}, f32[4,136,128]{2,1,0:T(8,128)S(1)}, u32[]{:S(2)}, u32[]{:S(2)}) collective-permute-start(f32[4,136,128]{2,1,0:T(8,128)S(1)} %pad_maximum_fusion.5), channel_id=1, source_target_pairs={{0,1},{1,0},{2,3},{3,2},{4,5},{5,4},{6,7},{7,6},{8,9},{9,8},{10,11... | collective-permute-start | bytes 835592 | tf_op jit(solution)/shard_map/ppermute | solution.py:260
  23.2 0.0 collective-permute-done.3
  23.3 0.0 copy-start.1
  23.3 0.0 copy-start.2
  23.3 1.6 %collective-permute-done.11 = f32[4,136,128]{2,1,0:T(8,128)S(1)} collective-permute-done((f32[4,136,128]{2,1,0:T(8,128)S(1)}, f32[4,136,128]{2,1,0:T(8,128)S(1)}, u32[]{:S(2)}, u32[]{:S(2)}) %collective-permute-start.11) | collective-permute-done | bytes 278560 | tf_op jit(solution)/shard_map/ppermute | solution.py:260
  24.9 0.1 pad_maximum_fusion.2.refs_2_
  25.0 0.0 collective-permute-done.7
  25.1 0.0 copy-done.1
  25.1 0.0 copy-done.2
  25.1 11.0 %purify.1 = f32[128,256]{1,0:T(8,128)} custom-call(f32[8,136,128]{2,1,0:T(8,128)S(1)} %pad_maximum_fusion.refs_0_, f32[16,136,128]{2,1,0:T(8,128)S(1)} %constant_dynamic-update-slice_fusion.refs_1_, f32[8,136,128]{2,1,0:T(8,128)S(1)} %pad_maximum_fusion.2.refs_2_, s32[16,9]{1,0:T(8,128)S(1)} %copy-done.1, s32[1,16]{1,0:T(1,128)S(1)} %bitcast.9), custom_call_target="tpu_custom_call" | custom-call | tf_op jit(solution)/shard_map/purify/pallas_call | solution.py:288
  (13 shorter events, 0.3 us)
Async XLA Ops:
  0.0 0.9 %copy-start = (f32[128,256]{1,0:T(8,128)S(1)}, f32[128,256]{1,0:T(8,128)}, u32[]{:S(2)}) copy-start(f32[128,256]{1,0:T(8,128)} %x_ref.1) | copy-start | bytes 393220
  0.9 7.3 %collective-permute-start.1 = (f32[136,128]{1,0:T(8,128)S(1)}, f32[136,128]{1,0:T(8,128)S(1)}, u32[]{:S(2)}, u32[]{:S(2)}) collective-permute-start(f32[136,128]{1,0:T(8,128)S(1)} %pack.1), channel_id=1, source_target_pairs={{0,16},{1,17},{2,18},{3,19},{4,20},{5,21},{6,22},{7,23},{8,24},{9,... | collective-permute-start | bytes 208904 | tf_op jit(solution)/shard_map/ppermute | solution.py:260
  4.9 4.3 %collective-permute-start.4 = (f32[136,128]{1,0:T(8,128)S(1)}, f32[136,128]{1,0:T(8,128)S(1)}, u32[]{:S(2)}, u32[]{:S(2)}) collective-permute-start(f32[136,128]{1,0:T(8,128)S(1)} %pack.1), channel_id=1, source_target_pairs={{0,8},{1,9},{2,10},{3,11},{4,12},{5,13},{6,14},{7,15},{8,0},{9,1},... | collective-permute-start | bytes 208904 | tf_op jit(solution)/shard_map/ppermute | solution.py:260
  6.5 6.1 %collective-permute-start.8 = (f32[136,128]{1,0:T(8,128)S(1)}, f32[136,128]{1,0:T(8,128)S(1)}, u32[]{:S(2)}, u32[]{:S(2)}) collective-permute-start(f32[136,128]{1,0:T(8,128)S(1)} %pack.1), channel_id=1, source_target_pairs={{0,24},{1,25},{2,26},{3,27},{4,28},{5,29},{6,30},{7,31},{8,16},{9,... | collective-permute-start | bytes 208904 | tf_op jit(solution)/shard_map/ppermute | solution.py:260
  6.5 7.6 %collective-permute-start = (f32[1,136,128]{2,1,0:T(8,128)S(1)}, f32[1,136,128]{2,1,0:T(8,128)S(1)}, u32[]{:S(2)}, u32[]{:S(2)}) collective-permute-start(f32[1,136,128]{2,1,0:T(8,128)S(1)} %bitcast.7), channel_id=1, source_target_pairs={{0,4},{1,3},{2,6},{3,1},{4,0},{5,7},{6,2},{7,5},{8,12},{9,11},{10,... | collective-permute-start | bytes 208904 | tf_op jit(solution)/shard_map/ppermute | solution.py:260
  9.3 6.5 %collective-permute-start.5 = (f32[2,136,128]{2,1,0:T(8,128)S(1)}, f32[2,136,128]{2,1,0:T(8,128)S(1)}, u32[]{:S(2)}, u32[]{:S(2)}) collective-permute-start(f32[2,136,128]{2,1,0:T(8,128)S(1)} %pad_maximum_fusion.7), channel_id=1, source_target_pairs={{0,2},{1,5},{2,0},{3,7},{4,6},{5,1},{6,4},{7,3},{8,10},{9,13},{10,... | collective-permute-start | bytes 417800 | tf_op jit(solution)/shard_map/ppermute | solution.py:260
  12.6 4.4 %collective-permute-start.9 = (f32[1,136,128]{2,1,0:T(8,128)S(1)}, f32[1,136,128]{2,1,0:T(8,128)S(1)}, u32[]{:S(2)}, u32[]{:S(2)}) collective-permute-start(f32[1,136,128]{2,1,0:T(8,128)S(1)} %bitcast.16), channel_id=1, source_target_pairs={{0,4},{1,3},{2,6},{3,1},{4,0},{5,7},{6,2},{7,5},{8,12},{9,11},{10,... | collective-permute-start | bytes 208904 | tf_op jit(solution)/shard_map/ppermute | solution.py:260
  14.1 6.5 %collective-permute-start.2 = (f32[2,136,128]{2,1,0:T(8,128)S(1)}, f32[2,136,128]{2,1,0:T(8,128)S(1)}, u32[]{:S(2)}, u32[]{:S(2)}) collective-permute-start(f32[2,136,128]{2,1,0:T(8,128)S(1)} %pad_maximum_fusion.6), channel_id=1, source_target_pairs={{0,2},{1,5},{2,0},{3,7},{4,6},{5,1},{6,4},{7,3},{8,10},{9,13},{10,... | collective-permute-start | bytes 417800 | tf_op jit(solution)/shard_map/ppermute | solution.py:260
  15.9 6.6 %collective-permute-start.6 = (f32[4,136,128]{2,1,0:T(8,128)S(1)}, f32[4,136,128]{2,1,0:T(8,128)S(1)}, u32[]{:S(2)}, u32[]{:S(2)}) collective-permute-start(f32[4,136,128]{2,1,0:T(8,128)S(1)} %pad_maximum_fusion.4), channel_id=1, source_target_pairs={{0,4},{1,3},{2,6},{3,1},{4,0},{5,7},{6,2},{7,5},{8,12},{9,11},{10,... | collective-permute-start | bytes 835592 | tf_op jit(solution)/shard_map/ppermute | solution.py:260
  17.0 5.6 %collective-permute-start.10 = (f32[2,136,128]{2,1,0:T(8,128)S(1)}, f32[2,136,128]{2,1,0:T(8,128)S(1)}, u32[]{:S(2)}, u32[]{:S(2)}) collective-permute-start(f32[2,136,128]{2,1,0:T(8,128)S(1)} %pad_maximum_fusion.8), channel_id=1, source_target_pairs={{0,2},{1,5},{2,0},{3,7},{4,6},{5,1},{6,4},{7,3},{8,10},{9,13},{10,... | collective-permute-start | bytes 417800 | tf_op jit(solution)/shard_map/ppermute | solution.py:260
  20.7 2.6 %collective-permute-start.3 = (f32[4,136,128]{2,1,0:T(8,128)S(1)}, f32[4,136,128]{2,1,0:T(8,128)S(1)}, u32[]{:S(2)}, u32[]{:S(2)}) collective-permute-start(f32[4,136,128]{2,1,0:T(8,128)S(1)} %pad_maximum_fusion.3), channel_id=1, source_target_pairs={{0,1},{1,0},{2,3},{3,2},{4,5},{5,4},{6,7},{7,6},{8,9},{9,8},{10,11... | collective-permute-start | bytes 835592 | tf_op jit(solution)/shard_map/ppermute | solution.py:260
  22.5 2.5 %collective-permute-start.7 = (f32[8,136,128]{2,1,0:T(8,128)S(1)}, f32[8,136,128]{2,1,0:T(8,128)S(1)}, u32[]{:S(2)}, u32[]{:S(2)}) collective-permute-start(f32[8,136,128]{2,1,0:T(8,128)S(1)} %pad_maximum_fusion.1), channel_id=1, source_target_pairs={{0,1},{1,0},{2,3},{3,2},{4,5},{5,4},{6,7},{7,6},{8,9},{9,8},{10,11... | collective-permute-start | bytes 1671176 | tf_op jit(solution)/shard_map/ppermute | solution.py:260
  22.6 2.3 %collective-permute-start.11 = (f32[4,136,128]{2,1,0:T(8,128)S(1)}, f32[4,136,128]{2,1,0:T(8,128)S(1)}, u32[]{:S(2)}, u32[]{:S(2)}) collective-permute-start(f32[4,136,128]{2,1,0:T(8,128)S(1)} %pad_maximum_fusion.5), channel_id=1, source_target_pairs={{0,1},{1,0},{2,3},{3,2},{4,5},{5,4},{6,7},{7,6},{8,9},{9,8},{10,11... | collective-permute-start | bytes 835592 | tf_op jit(solution)/shard_map/ppermute | solution.py:260
  23.3 1.8 %copy-start.1 = (s32[16,9]{1,0:T(8,128)S(1)}, s32[16,9]{1,0:T(8,128)}, u32[]{:S(2)}) copy-start(s32[16,9]{1,0:T(8,128)} %refs_3_.1) | copy-start | bytes 1732
  23.3 1.8 %copy-start.2 = (s32[16]{0:T(128)S(1)}, s32[16]{0:T(128)}, u32[]{:S(2)}) copy-start(s32[16]{0:T(128)} %param.5) | copy-start | bytes 196

commit v6 on v5

--- a/solution.py
+++ b/solution.py
@@ -84,6 +84,10 @@
     return 1 - group % 2
 
 
+def form(d, a):
+    return (d & 1 & (a ^ a >> 1)) ^ (d >> 1 & a >> 1)
+
+
 def place(reps_n):
     rank = lax.axis_index("col") * reps_n + lax.axis_index("rep")
     return rank // 2, rank & 1, lax.axis_index("row")
@@ -95,7 +99,7 @@
 
     @pl.when(big_row != big_col)
     def _():
-        pick = jnp.where(big_row < big_col, core, 1 - core)
+        pick = core ^ form(big_row ^ big_col, big_row)
         out_ref[:side, :] = x_ref[:, pl.ds(pl.multiple_of(pick * side, side), side)]
         out_ref[side:, :] = jnp.zeros((EXTRA, side), jnp.float32)
 
@@ -109,10 +113,17 @@
         out_ref[side:, :] = jnp.broadcast_to(diagonal, (EXTRA, side))
 
 
-def write_mask(pattern_ref, order_ref, hits):
+def write_mask(pattern_ref, order_ref, hits, bigs, base):
     blocks, total = hits.shape
-    lane_block = lax.broadcasted_iota(jnp.int32, (1, total), 1) // (total // blocks)
-    row_block = lax.broadcasted_iota(jnp.int32, (blocks, 1), 0)
+    per = blocks // bigs
+    half = per // 2
+
+    def actual(index):
+        big, within = index // per, index % per
+        return (big ^ base) * per + ((within // half) ^ form(big, base)) * half + within % half
+
+    lane_block = actual(lax.broadcasted_iota(jnp.int32, (1, total), 1) // (total // blocks))
+    row_block = actual(lax.broadcasted_iota(jnp.int32, (blocks, 1), 0))
     natural_col = jnp.zeros((1, total), jnp.int32)
     natural_row = jnp.zeros((blocks, 1), jnp.int32)
     for b in range(blocks):
@@ -143,21 +154,16 @@
 
     rank = big_row * 2 + core
 
-    def chunk(a, core_of, b, rows):
-        away = rank ^ (a * 2 + core_of)
+    def chunk(a, half, b, rows):
+        away = rank ^ ((a ^ big_col) * 2 + (half ^ form(a, big_col)))
+        (index, group), = [(index, group) for index, group in enumerate(groups) if b in group]
         swapped = away & 1
-        result = None
-        for index, group in enumerate(groups):
-            order = core ^ swapped ^ flipped(index)
-            bits = swapped << links
-            for step in range(links):
-                bit = jnp.where(order == 0, (away >> (1 + step)) & 1, (away >> (links - step)) & 1)
-                bits = bits | (bit << step)
-            chain = big_col ^ b
-            member = jnp.clip(chain - group[0], 0, len(group) - 1)
-            value = held[index][bits * len(group) + member, rows, :]
-            result = value if result is None else jnp.where(chain >= group[0], value, result)
-        return result
+        order = core ^ swapped ^ flipped(index)
+        bits = swapped << links
+        for step in range(links):
+            bit = jnp.where(order == 0, (away >> (1 + step)) & 1, (away >> (links - step)) & 1)
+            bits = bits | (bit << step)
+        return held[index][bits * len(group) + group.index(b), rows, :]
 
     def put(h, l, value, r, c):
         high, low = split(value)
@@ -173,11 +179,12 @@
     def unpack(a, b):
         if a != b:
             for j in range(2):
-                k = j if a < b else 1 - j
+                k = j ^ form(a ^ b, a)
                 value = chunk(a, j, b, slice(0, side))
                 r, c = span(2 * a + j, side), span(2 * b + k, side)
-                put(xh, xl, value, r, c)
-                put(xh, xl, value.T, c, r)
+                high, low = split(value)
+                xh[r, c], xl[r, c] = high, low
+                xh[c, r], xl[c, r] = high.T, low.T
             return
         i, j = iotas(side)
         m0 = chunk(a, 0, a, slice(0, side))
@@ -197,11 +204,13 @@
         return jnp.concatenate(parts, axis=0)
 
     def mirrored(h, l, value, a, b):
-        put(h, l, value, span(a, wide), span(b, wide))
+        high, low = split(value)
+        r, c = span(a, wide), span(b, wide)
+        h[r, c], l[r, c] = high, low
         if a != b:
-            put(h, l, value.T, span(b, wide), span(a, wide))
-
-    write_mask(pattern_ref, order_ref, hits)
+            h[c, r], l[c, r] = high.T, low.T
+
+    write_mask(pattern_ref, order_ref, hits, bigs, big_col)
 
     for b in reversed(range(bigs)):
         for a in reversed(range(b + 1)):
@@ -223,8 +232,10 @@
             value = 3.0 * (xh[r, c].astype(jnp.float32) + xl[r, c].astype(jnp.float32)) - 2.0 * square
             mirrored(zh, zl, value, a, b)
 
-    cols = at(big_col, wide)
-    rows = at(rank, side)
+    cols = span(0, wide)
+    own = big_row ^ big_col
+    own_rank = own * 2 + (core ^ form(own, big_col))
+    rows = at(own_rank, side)
 
     def term(k):
         r = span(k, wide)
@@ -242,7 +253,7 @@
     value = 3.0 * (ch[rows, :].astype(jnp.float32) + cl[rows, :].astype(jnp.float32)) - 2.0 * square
     vh, vl = split(value)
     result = product(vh, vl, ch[:, cols], cl[:, cols])
-    out_ref[...] = masked(result, rank * (side // block), cols)
+    out_ref[...] = masked(result, own_rank * (side // block), cols)
 
 
 def whole(shape, density, pattern, grid_order):
@@ -301,7 +312,7 @@
     sizes = [shape[name] for name in AXES]
     powers = all(size & (size - 1) == 0 for size in sizes)
     ranks = sizes[1] * sizes[2]
-    squares = wide == 2 * side and side % 128 == 0 and sizes[0] * 2 == ranks
+    squares = wide == 2 * side and side % 128 == 0 and sizes[0] * 2 == ranks and sizes[0] <= 4
     return powers and squares and total * total * 24 <= WORK_BYTES
 
 

time: 36.2 us -> 36 us (level)
  no operation moved by 1% of the time
where the time goes in v6:
time: 36 us; the launch traced here: 35.9 us
  starting transfers between devices  15.3 us (42%)
  Pallas kernels  10.8 us (30%)
  waiting for transfers between devices  8.33 us (23%)
  local copies, waits for them, and re-layouts  1 us (3%)
    ppermute x12, starting transfers between devices, swap(): return lax.ppermute(value, AXES, pairs)  15.3 us
    pallas_call x1, Pallas kernels, whole(): pl.pallas_call(functools.partial(work_kernel, (rows_n, ranks, reps_n)), o...  10.8 us
    ppermute x12, waiting for transfers between devices, swap(): return lax.ppermute(value, AXES, pairs)  8.33 us
    unnamed x10, local copies, waits for them, and re-layouts  0.96 us
  transfers between devices with their start and end apart: 12, of which 6 were waited for; matrix products, arithmetic and copies ran while one was open for 1% of the time, Pallas kernels for 0%

profile of v6, /device:TPU:0, one launch (start us, length us, event | category | flops | bytes accessed | tf_op | source)
XLA Modules:
  0.0 35.9 jit_solution(5421399876848490279)
XLA Ops:
  0.0 0.0 copy-start
  0.0 0.9 %copy-done = f32[128,256]{1,0:T(8,128)S(1)} copy-done((f32[128,256]{1,0:T(8,128)S(1)}, f32[128,256]{1,0:T(8,128)}, u32[]{:S(2)}) %copy-start) | copy-done | bytes 131096
  0.9 4.0 %collective-permute-start.1 = (f32[136,128]{1,0:T(8,128)S(1)}, f32[136,128]{1,0:T(8,128)S(1)}, u32[]{:S(2)}, u32[]{:S(2)}) collective-permute-start(f32[136,128]{1,0:T(8,128)S(1)} %pack.1), channel_id=1, source_target_pairs={{0,16},{1,17},{2,18},{3,19},{4,20},{5,21},{6,22},{7,23},{8,24},{9,... | collective-permute-start | bytes 208904 | tf_op jit(solution)/shard_map/ppermute | solution.py:271
  4.9 1.6 %collective-permute-start.4 = (f32[136,128]{1,0:T(8,128)S(1)}, f32[136,128]{1,0:T(8,128)S(1)}, u32[]{:S(2)}, u32[]{:S(2)}) collective-permute-start(f32[136,128]{1,0:T(8,128)S(1)} %pack.1), channel_id=1, source_target_pairs={{0,8},{1,9},{2,10},{3,11},{4,12},{5,13},{6,14},{7,15},{8,0},{9,1},... | collective-permute-start | bytes 208904 | tf_op jit(solution)/shard_map/ppermute | solution.py:271
  6.5 0.0 collective-permute-start.8
  6.5 1.7 %collective-permute-start = (f32[1,136,128]{2,1,0:T(8,128)S(1)}, f32[1,136,128]{2,1,0:T(8,128)S(1)}, u32[]{:S(2)}, u32[]{:S(2)}) collective-permute-start(f32[1,136,128]{2,1,0:T(8,128)S(1)} %bitcast.7), channel_id=1, source_target_pairs={{0,4},{1,3},{2,6},{3,1},{4,0},{5,7},{6,2},{7,5},{8,12},{9,11},{10,... | collective-permute-start | bytes 208904 | tf_op jit(solution)/shard_map/ppermute | solution.py:271
  8.2 0.0 collective-permute-done.1
  8.2 1.0 %collective-permute-done.4 = f32[136,128]{1,0:T(8,128)S(1)} collective-permute-done((f32[136,128]{1,0:T(8,128)S(1)}, f32[136,128]{1,0:T(8,128)S(1)}, u32[]{:S(2)}, u32[]{:S(2)}) %collective-permute-start.4) | collective-permute-done | bytes 69664 | tf_op jit(solution)/shard_map/ppermute | solution.py:271
  9.3 1.7 %collective-permute-start.5 = (f32[2,136,128]{2,1,0:T(8,128)S(1)}, f32[2,136,128]{2,1,0:T(8,128)S(1)}, u32[]{:S(2)}, u32[]{:S(2)}) collective-permute-start(f32[2,136,128]{2,1,0:T(8,128)S(1)} %pad_maximum_fusion.7), channel_id=1, source_target_pairs={{0,2},{1,5},{2,0},{3,7},{4,6},{5,1},{6,4},{7,3},{8,10},{9,13},{10,... | collective-permute-start | bytes 417800 | tf_op jit(solution)/shard_map/ppermute | solution.py:271
  10.9 1.7 %collective-permute-done.8 = f32[136,128]{1,0:T(8,128)S(1)} collective-permute-done((f32[136,128]{1,0:T(8,128)S(1)}, f32[136,128]{1,0:T(8,128)S(1)}, u32[]{:S(2)}, u32[]{:S(2)}) %collective-permute-start.8) | collective-permute-done | bytes 69664 | tf_op jit(solution)/shard_map/ppermute | solution.py:271
  12.6 1.5 %collective-permute-start.9 = (f32[1,136,128]{2,1,0:T(8,128)S(1)}, f32[1,136,128]{2,1,0:T(8,128)S(1)}, u32[]{:S(2)}, u32[]{:S(2)}) collective-permute-start(f32[1,136,128]{2,1,0:T(8,128)S(1)} %bitcast.16), channel_id=1, source_target_pairs={{0,4},{1,3},{2,6},{3,1},{4,0},{5,7},{6,2},{7,5},{8,12},{9,11},{10,... | collective-permute-start | bytes 208904 | tf_op jit(solution)/shard_map/ppermute | solution.py:271
  14.1 0.0 collective-permute-done
  14.1 1.7 %collective-permute-start.2 = (f32[2,136,128]{2,1,0:T(8,128)S(1)}, f32[2,136,128]{2,1,0:T(8,128)S(1)}, u32[]{:S(2)}, u32[]{:S(2)}) collective-permute-start(f32[2,136,128]{2,1,0:T(8,128)S(1)} %pad_maximum_fusion.6), channel_id=1, source_target_pairs={{0,2},{1,5},{2,0},{3,7},{4,6},{5,1},{6,4},{7,3},{8,10},{9,13},{10,... | collective-permute-start | bytes 417800 | tf_op jit(solution)/shard_map/ppermute | solution.py:271
  15.8 0.0 collective-permute-done.5
  15.9 1.0 %collective-permute-start.6 = (f32[4,136,128]{2,1,0:T(8,128)S(1)}, f32[4,136,128]{2,1,0:T(8,128)S(1)}, u32[]{:S(2)}, u32[]{:S(2)}) collective-permute-start(f32[4,136,128]{2,1,0:T(8,128)S(1)} %pad_maximum_fusion.4), channel_id=1, source_target_pairs={{0,4},{1,3},{2,6},{3,1},{4,0},{5,7},{6,2},{7,5},{8,12},{9,11},{10,... | collective-permute-start | bytes 835592 | tf_op jit(solution)/shard_map/ppermute | solution.py:271
  16.9 0.2 collective-permute-done.9
  17.0 1.5 %collective-permute-start.10 = (f32[2,136,128]{2,1,0:T(8,128)S(1)}, f32[2,136,128]{2,1,0:T(8,128)S(1)}, u32[]{:S(2)}, u32[]{:S(2)}) collective-permute-start(f32[2,136,128]{2,1,0:T(8,128)S(1)} %pad_maximum_fusion.8), channel_id=1, source_target_pairs={{0,2},{1,5},{2,0},{3,7},{4,6},{5,1},{6,4},{7,3},{8,10},{9,13},{10,... | collective-permute-start | bytes 417800 | tf_op jit(solution)/shard_map/ppermute | solution.py:271
  18.5 2.1 %collective-permute-done.2 = f32[2,136,128]{2,1,0:T(8,128)S(1)} collective-permute-done((f32[2,136,128]{2,1,0:T(8,128)S(1)}, f32[2,136,128]{2,1,0:T(8,128)S(1)}, u32[]{:S(2)}, u32[]{:S(2)}) %collective-permute-start.2) | collective-permute-done | bytes 139296 | tf_op jit(solution)/shard_map/ppermute | solution.py:271
  20.7 0.1 collective-permute-start.3
  20.8 1.7 %collective-permute-done.6 = f32[4,136,128]{2,1,0:T(8,128)S(1)} collective-permute-done((f32[4,136,128]{2,1,0:T(8,128)S(1)}, f32[4,136,128]{2,1,0:T(8,128)S(1)}, u32[]{:S(2)}, u32[]{:S(2)}) %collective-permute-start.6) | collective-permute-done | bytes 278560 | tf_op jit(solution)/shard_map/ppermute | solution.py:271
  22.5 0.1 pad_maximum_fusion.1
  22.5 0.1 collective-permute-start.7
  22.6 0.0 collective-permute-done.10
  22.6 0.6 %collective-permute-start.11 = (f32[4,136,128]{2,1,0:T(8,128)S(1)}, f32[4,136,128]{2,1,0:T(8,128)S(1)}, u32[]{:S(2)}, u32[]{:S(2)}) collective-permute-start(f32[4,136,128]{2,1,0:T(8,128)S(1)} %pad_maximum_fusion.5), channel_id=1, source_target_pairs={{0,1},{1,0},{2,3},{3,2},{4,5},{5,4},{6,7},{7,6},{8,9},{9,8},{10,11... | collective-permute-start | bytes 835592 | tf_op jit(solution)/shard_map/ppermute | solution.py:271
  23.2 0.0 collective-permute-done.3
  23.3 0.0 copy-start.1
  23.3 0.0 copy-start.2
  23.3 1.6 %collective-permute-done.11 = f32[4,136,128]{2,1,0:T(8,128)S(1)} collective-permute-done((f32[4,136,128]{2,1,0:T(8,128)S(1)}, f32[4,136,128]{2,1,0:T(8,128)S(1)}, u32[]{:S(2)}, u32[]{:S(2)}) %collective-permute-start.11) | collective-permute-done | bytes 278560 | tf_op jit(solution)/shard_map/ppermute | solution.py:271
  24.9 0.1 pad_maximum_fusion.2.refs_2_
  25.0 0.0 collective-permute-done.7
  25.1 0.0 copy-done.1
  25.1 0.0 copy-done.2
  25.1 10.8 %purify.1 = f32[128,256]{1,0:T(8,128)} custom-call(f32[8,136,128]{2,1,0:T(8,128)S(1)} %pad_maximum_fusion.refs_0_, f32[16,136,128]{2,1,0:T(8,128)S(1)} %constant_dynamic-update-slice_fusion.refs_1_, f32[8,136,128]{2,1,0:T(8,128)S(1)} %pad_maximum_fusion.2.refs_2_, s32[16,9]{1,0:T(8,128)S(1)} %copy-done.1, s32[1,16]{1,0:T(1,128)S(1)} %bitcast.9), custom_call_target="tpu_custom_call" | custom-call | tf_op jit(solution)/shard_map/purify/pallas_call | solution.py:299
  (13 shorter events, 0.3 us)
Async XLA Ops:
  0.0 0.9 %copy-start = (f32[128,256]{1,0:T(8,128)S(1)}, f32[128,256]{1,0:T(8,128)}, u32[]{:S(2)}) copy-start(f32[128,256]{1,0:T(8,128)} %x_ref.1) | copy-start | bytes 393220
  0.9 7.3 %collective-permute-start.1 = (f32[136,128]{1,0:T(8,128)S(1)}, f32[136,128]{1,0:T(8,128)S(1)}, u32[]{:S(2)}, u32[]{:S(2)}) collective-permute-start(f32[136,128]{1,0:T(8,128)S(1)} %pack.1), channel_id=1, source_target_pairs={{0,16},{1,17},{2,18},{3,19},{4,20},{5,21},{6,22},{7,23},{8,24},{9,... | collective-permute-start | bytes 208904 | tf_op jit(solution)/shard_map/ppermute | solution.py:271
  4.9 4.3 %collective-permute-start.4 = (f32[136,128]{1,0:T(8,128)S(1)}, f32[136,128]{1,0:T(8,128)S(1)}, u32[]{:S(2)}, u32[]{:S(2)}) collective-permute-start(f32[136,128]{1,0:T(8,128)S(1)} %pack.1), channel_id=1, source_target_pairs={{0,8},{1,9},{2,10},{3,11},{4,12},{5,13},{6,14},{7,15},{8,0},{9,1},... | collective-permute-start | bytes 208904 | tf_op jit(solution)/shard_map/ppermute | solution.py:271
  6.5 6.1 %collective-permute-start.8 = (f32[136,128]{1,0:T(8,128)S(1)}, f32[136,128]{1,0:T(8,128)S(1)}, u32[]{:S(2)}, u32[]{:S(2)}) collective-permute-start(f32[136,128]{1,0:T(8,128)S(1)} %pack.1), channel_id=1, source_target_pairs={{0,24},{1,25},{2,26},{3,27},{4,28},{5,29},{6,30},{7,31},{8,16},{9,... | collective-permute-start | bytes 208904 | tf_op jit(solution)/shard_map/ppermute | solution.py:271
  6.5 7.6 %collective-permute-start = (f32[1,136,128]{2,1,0:T(8,128)S(1)}, f32[1,136,128]{2,1,0:T(8,128)S(1)}, u32[]{:S(2)}, u32[]{:S(2)}) collective-permute-start(f32[1,136,128]{2,1,0:T(8,128)S(1)} %bitcast.7), channel_id=1, source_target_pairs={{0,4},{1,3},{2,6},{3,1},{4,0},{5,7},{6,2},{7,5},{8,12},{9,11},{10,... | collective-permute-start | bytes 208904 | tf_op jit(solution)/shard_map/ppermute | solution.py:271
  9.3 6.5 %collective-permute-start.5 = (f32[2,136,128]{2,1,0:T(8,128)S(1)}, f32[2,136,128]{2,1,0:T(8,128)S(1)}, u32[]{:S(2)}, u32[]{:S(2)}) collective-permute-start(f32[2,136,128]{2,1,0:T(8,128)S(1)} %pad_maximum_fusion.7), channel_id=1, source_target_pairs={{0,2},{1,5},{2,0},{3,7},{4,6},{5,1},{6,4},{7,3},{8,10},{9,13},{10,... | collective-permute-start | bytes 417800 | tf_op jit(solution)/shard_map/ppermute | solution.py:271
  12.6 4.4 %collective-permute-start.9 = (f32[1,136,128]{2,1,0:T(8,128)S(1)}, f32[1,136,128]{2,1,0:T(8,128)S(1)}, u32[]{:S(2)}, u32[]{:S(2)}) collective-permute-start(f32[1,136,128]{2,1,0:T(8,128)S(1)} %bitcast.16), channel_id=1, source_target_pairs={{0,4},{1,3},{2,6},{3,1},{4,0},{5,7},{6,2},{7,5},{8,12},{9,11},{10,... | collective-permute-start | bytes 208904 | tf_op jit(solution)/shard_map/ppermute | solution.py:271
  14.1 6.5 %collective-permute-start.2 = (f32[2,136,128]{2,1,0:T(8,128)S(1)}, f32[2,136,128]{2,1,0:T(8,128)S(1)}, u32[]{:S(2)}, u32[]{:S(2)}) collective-permute-start(f32[2,136,128]{2,1,0:T(8,128)S(1)} %pad_maximum_fusion.6), channel_id=1, source_target_pairs={{0,2},{1,5},{2,0},{3,7},{4,6},{5,1},{6,4},{7,3},{8,10},{9,13},{10,... | collective-permute-start | bytes 417800 | tf_op jit(solution)/shard_map/ppermute | solution.py:271
  15.9 6.6 %collective-permute-start.6 = (f32[4,136,128]{2,1,0:T(8,128)S(1)}, f32[4,136,128]{2,1,0:T(8,128)S(1)}, u32[]{:S(2)}, u32[]{:S(2)}) collective-permute-start(f32[4,136,128]{2,1,0:T(8,128)S(1)} %pad_maximum_fusion.4), channel_id=1, source_target_pairs={{0,4},{1,3},{2,6},{3,1},{4,0},{5,7},{6,2},{7,5},{8,12},{9,11},{10,... | collective-permute-start | bytes 835592 | tf_op jit(solution)/shard_map/ppermute | solution.py:271
  17.0 5.6 %collective-permute-start.10 = (f32[2,136,128]{2,1,0:T(8,128)S(1)}, f32[2,136,128]{2,1,0:T(8,128)S(1)}, u32[]{:S(2)}, u32[]{:S(2)}) collective-permute-start(f32[2,136,128]{2,1,0:T(8,128)S(1)} %pad_maximum_fusion.8), channel_id=1, source_target_pairs={{0,2},{1,5},{2,0},{3,7},{4,6},{5,1},{6,4},{7,3},{8,10},{9,13},{10,... | collective-permute-start | bytes 417800 | tf_op jit(solution)/shard_map/ppermute | solution.py:271
  20.7 2.6 %collective-permute-start.3 = (f32[4,136,128]{2,1,0:T(8,128)S(1)}, f32[4,136,128]{2,1,0:T(8,128)S(1)}, u32[]{:S(2)}, u32[]{:S(2)}) collective-permute-start(f32[4,136,128]{2,1,0:T(8,128)S(1)} %pad_maximum_fusion.3), channel_id=1, source_target_pairs={{0,1},{1,0},{2,3},{3,2},{4,5},{5,4},{6,7},{7,6},{8,9},{9,8},{10,11... | collective-permute-start | bytes 835592 | tf_op jit(solution)/shard_map/ppermute | solution.py:271
  22.5 2.5 %collective-permute-start.7 = (f32[8,136,128]{2,1,0:T(8,128)S(1)}, f32[8,136,128]{2,1,0:T(8,128)S(1)}, u32[]{:S(2)}, u32[]{:S(2)}) collective-permute-start(f32[8,136,128]{2,1,0:T(8,128)S(1)} %pad_maximum_fusion.1), channel_id=1, source_target_pairs={{0,1},{1,0},{2,3},{3,2},{4,5},{5,4},{6,7},{7,6},{8,9},{9,8},{10,11... | collective-permute-start | bytes 1671176 | tf_op jit(solution)/shard_map/ppermute | solution.py:271
  22.6 2.3 %collective-permute-start.11 = (f32[4,136,128]{2,1,0:T(8,128)S(1)}, f32[4,136,128]{2,1,0:T(8,128)S(1)}, u32[]{:S(2)}, u32[]{:S(2)}) collective-permute-start(f32[4,136,128]{2,1,0:T(8,128)S(1)} %pad_maximum_fusion.5), channel_id=1, source_target_pairs={{0,1},{1,0},{2,3},{3,2},{4,5},{5,4},{6,7},{7,6},{8,9},{9,8},{10,11... | collective-permute-start | bytes 835592 | tf_op jit(solution)/shard_map/ppermute | solution.py:271
  23.3 1.8 %copy-start.1 = (s32[16,9]{1,0:T(8,128)S(1)}, s32[16,9]{1,0:T(8,128)}, u32[]{:S(2)}) copy-start(s32[16,9]{1,0:T(8,128)} %refs_3_.1) | copy-start | bytes 1732
  23.3 1.8 %copy-start.2 = (s32[16]{0:T(128)S(1)}, s32[16]{0:T(128)}, u32[]{:S(2)}) copy-start(s32[16]{0:T(128)} %param.5) | copy-start | bytes 196

commit v7 on v6

--- a/solution.py
+++ b/solution.py
@@ -210,8 +210,6 @@
         if a != b:
             h[c, r], l[c, r] = high.T, low.T
 
-    write_mask(pattern_ref, order_ref, hits, bigs, big_col)
-
     for b in reversed(range(bigs)):
         for a in reversed(range(b + 1)):
             r, c = span(a, wide), span(b, wide)
@@ -232,6 +230,8 @@
             value = 3.0 * (xh[r, c].astype(jnp.float32) + xl[r, c].astype(jnp.float32)) - 2.0 * square
             mirrored(zh, zl, value, a, b)
 
+    write_mask(pattern_ref, order_ref, hits, bigs, big_col)
+
     cols = span(0, wide)
     own = big_row ^ big_col
     own_rank = own * 2 + (core ^ form(own, big_col))
@@ -281,7 +281,7 @@
     )(density)
     links = (ranks // 2).bit_length() - 1
     came = {0: mine[None]}
-    for away in range(1, rows_n):
+    for away in reversed(range(1, rows_n)):
         came[away] = swap(mine, lambda z, r: (z ^ away, r))[None]
     groups = chain_groups(rows_n)
     value = [jnp.concatenate([came[chain] for chain in group], axis=0) for group in groups]

time: 36 us -> 36 us (level)
  no operation moved by 1% of the time
where the time goes in v7:
time: 36 us; the launch traced here: 35.9 us
  starting transfers between devices  15.3 us (42%)
  Pallas kernels  10.8 us (30%)
  waiting for transfers between devices  8.33 us (23%)
  local copies, waits for them, and re-layouts  1 us (3%)
    ppermute x12, starting transfers between devices, swap(): return lax.ppermute(value, AXES, pairs)  15.3 us
    pallas_call x1, Pallas kernels, whole(): pl.pallas_call(functools.partial(work_kernel, (rows_n, ranks, reps_n)), o...  10.8 us
    ppermute x12, waiting for transfers between devices, swap(): return lax.ppermute(value, AXES, pairs)  8.33 us
    unnamed x10, local copies, waits for them, and re-layouts  0.96 us
  transfers between devices with their start and end apart: 12, of which 6 were waited for; matrix products, arithmetic and copies ran while one was open for 1% of the time, Pallas kernels for 0%

profile of v7, /device:TPU:0, one launch (start us, length us, event | category | flops | bytes accessed | tf_op | source)
XLA Modules:
  0.0 35.9 jit_solution(3237611581180074420)
XLA Ops:
  0.0 0.0 copy-start
  0.0 0.9 %copy-done = f32[128,256]{1,0:T(8,128)S(1)} copy-done((f32[128,256]{1,0:T(8,128)S(1)}, f32[128,256]{1,0:T(8,128)}, u32[]{:S(2)}) %copy-start) | copy-done | bytes 131096
  0.9 4.0 %collective-permute-start.1 = (f32[136,128]{1,0:T(8,128)S(1)}, f32[136,128]{1,0:T(8,128)S(1)}, u32[]{:S(2)}, u32[]{:S(2)}) collective-permute-start(f32[136,128]{1,0:T(8,128)S(1)} %pack.1), channel_id=1, source_target_pairs={{0,16},{1,17},{2,18},{3,19},{4,20},{5,21},{6,22},{7,23},{8,24},{9,... | collective-permute-start | bytes 208904 | tf_op jit(solution)/shard_map/ppermute | solution.py:271
  4.9 1.6 %collective-permute-start.4 = (f32[136,128]{1,0:T(8,128)S(1)}, f32[136,128]{1,0:T(8,128)S(1)}, u32[]{:S(2)}, u32[]{:S(2)}) collective-permute-start(f32[136,128]{1,0:T(8,128)S(1)} %pack.1), channel_id=1, source_target_pairs={{0,8},{1,9},{2,10},{3,11},{4,12},{5,13},{6,14},{7,15},{8,0},{9,1},... | collective-permute-start | bytes 208904 | tf_op jit(solution)/shard_map/ppermute | solution.py:271
  6.5 0.0 collective-permute-start.8
  6.5 1.7 %collective-permute-start = (f32[1,136,128]{2,1,0:T(8,128)S(1)}, f32[1,136,128]{2,1,0:T(8,128)S(1)}, u32[]{:S(2)}, u32[]{:S(2)}) collective-permute-start(f32[1,136,128]{2,1,0:T(8,128)S(1)} %bitcast.7), channel_id=1, source_target_pairs={{0,4},{1,3},{2,6},{3,1},{4,0},{5,7},{6,2},{7,5},{8,12},{9,11},{10,... | collective-permute-start | bytes 208904 | tf_op jit(solution)/shard_map/ppermute | solution.py:271
  8.2 0.0 collective-permute-done.1
  8.2 1.0 %collective-permute-done.4 = f32[136,128]{1,0:T(8,128)S(1)} collective-permute-done((f32[136,128]{1,0:T(8,128)S(1)}, f32[136,128]{1,0:T(8,128)S(1)}, u32[]{:S(2)}, u32[]{:S(2)}) %collective-permute-start.4) | collective-permute-done | bytes 69664 | tf_op jit(solution)/shard_map/ppermute | solution.py:271
  9.3 1.7 %collective-permute-start.5 = (f32[2,136,128]{2,1,0:T(8,128)S(1)}, f32[2,136,128]{2,1,0:T(8,128)S(1)}, u32[]{:S(2)}, u32[]{:S(2)}) collective-permute-start(f32[2,136,128]{2,1,0:T(8,128)S(1)} %pad_maximum_fusion.7), channel_id=1, source_target_pairs={{0,2},{1,5},{2,0},{3,7},{4,6},{5,1},{6,4},{7,3},{8,10},{9,13},{10,... | collective-permute-start | bytes 417800 | tf_op jit(solution)/shard_map/ppermute | solution.py:271
  10.9 1.7 %collective-permute-done.8 = f32[136,128]{1,0:T(8,128)S(1)} collective-permute-done((f32[136,128]{1,0:T(8,128)S(1)}, f32[136,128]{1,0:T(8,128)S(1)}, u32[]{:S(2)}, u32[]{:S(2)}) %collective-permute-start.8) | collective-permute-done | bytes 69664 | tf_op jit(solution)/shard_map/ppermute | solution.py:271
  12.6 1.5 %collective-permute-start.9 = (f32[1,136,128]{2,1,0:T(8,128)S(1)}, f32[1,136,128]{2,1,0:T(8,128)S(1)}, u32[]{:S(2)}, u32[]{:S(2)}) collective-permute-start(f32[1,136,128]{2,1,0:T(8,128)S(1)} %bitcast.16), channel_id=1, source_target_pairs={{0,4},{1,3},{2,6},{3,1},{4,0},{5,7},{6,2},{7,5},{8,12},{9,11},{10,... | collective-permute-start | bytes 208904 | tf_op jit(solution)/shard_map/ppermute | solution.py:271
  14.1 0.0 collective-permute-done
  14.1 1.7 %collective-permute-start.2 = (f32[2,136,128]{2,1,0:T(8,128)S(1)}, f32[2,136,128]{2,1,0:T(8,128)S(1)}, u32[]{:S(2)}, u32[]{:S(2)}) collective-permute-start(f32[2,136,128]{2,1,0:T(8,128)S(1)} %pad_maximum_fusion.6), channel_id=1, source_target_pairs={{0,2},{1,5},{2,0},{3,7},{4,6},{5,1},{6,4},{7,3},{8,10},{9,13},{10,... | collective-permute-start | bytes 417800 | tf_op jit(solution)/shard_map/ppermute | solution.py:271
  15.8 0.0 collective-permute-done.5
  15.9 1.0 %collective-permute-start.6 = (f32[4,136,128]{2,1,0:T(8,128)S(1)}, f32[4,136,128]{2,1,0:T(8,128)S(1)}, u32[]{:S(2)}, u32[]{:S(2)}) collective-permute-start(f32[4,136,128]{2,1,0:T(8,128)S(1)} %pad_maximum_fusion.4), channel_id=1, source_target_pairs={{0,4},{1,3},{2,6},{3,1},{4,0},{5,7},{6,2},{7,5},{8,12},{9,11},{10,... | collective-permute-start | bytes 835592 | tf_op jit(solution)/shard_map/ppermute | solution.py:271
  16.9 0.2 collective-permute-done.9
  17.0 1.5 %collective-permute-start.10 = (f32[2,136,128]{2,1,0:T(8,128)S(1)}, f32[2,136,128]{2,1,0:T(8,128)S(1)}, u32[]{:S(2)}, u32[]{:S(2)}) collective-permute-start(f32[2,136,128]{2,1,0:T(8,128)S(1)} %pad_maximum_fusion.8), channel_id=1, source_target_pairs={{0,2},{1,5},{2,0},{3,7},{4,6},{5,1},{6,4},{7,3},{8,10},{9,13},{10,... | collective-permute-start | bytes 417800 | tf_op jit(solution)/shard_map/ppermute | solution.py:271
  18.5 2.1 %collective-permute-done.2 = f32[2,136,128]{2,1,0:T(8,128)S(1)} collective-permute-done((f32[2,136,128]{2,1,0:T(8,128)S(1)}, f32[2,136,128]{2,1,0:T(8,128)S(1)}, u32[]{:S(2)}, u32[]{:S(2)}) %collective-permute-start.2) | collective-permute-done | bytes 139296 | tf_op jit(solution)/shard_map/ppermute | solution.py:271
  20.7 0.1 collective-permute-start.3
  20.8 1.7 %collective-permute-done.6 = f32[4,136,128]{2,1,0:T(8,128)S(1)} collective-permute-done((f32[4,136,128]{2,1,0:T(8,128)S(1)}, f32[4,136,128]{2,1,0:T(8,128)S(1)}, u32[]{:S(2)}, u32[]{:S(2)}) %collective-permute-start.6) | collective-permute-done | bytes 278560 | tf_op jit(solution)/shard_map/ppermute | solution.py:271
  22.5 0.1 pad_maximum_fusion.1
  22.5 0.1 collective-permute-start.7
  22.6 0.0 collective-permute-done.10
  22.6 0.6 %collective-permute-start.11 = (f32[4,136,128]{2,1,0:T(8,128)S(1)}, f32[4,136,128]{2,1,0:T(8,128)S(1)}, u32[]{:S(2)}, u32[]{:S(2)}) collective-permute-start(f32[4,136,128]{2,1,0:T(8,128)S(1)} %pad_maximum_fusion.5), channel_id=1, source_target_pairs={{0,1},{1,0},{2,3},{3,2},{4,5},{5,4},{6,7},{7,6},{8,9},{9,8},{10,11... | collective-permute-start | bytes 835592 | tf_op jit(solution)/shard_map/ppermute | solution.py:271
  23.2 0.0 collective-permute-done.3
  23.3 0.0 copy-start.1
  23.3 0.0 copy-start.2
  23.3 1.6 %collective-permute-done.11 = f32[4,136,128]{2,1,0:T(8,128)S(1)} collective-permute-done((f32[4,136,128]{2,1,0:T(8,128)S(1)}, f32[4,136,128]{2,1,0:T(8,128)S(1)}, u32[]{:S(2)}, u32[]{:S(2)}) %collective-permute-start.11) | collective-permute-done | bytes 278560 | tf_op jit(solution)/shard_map/ppermute | solution.py:271
  24.9 0.1 pad_maximum_fusion.2.refs_2_
  25.0 0.0 collective-permute-done.7
  25.1 0.0 copy-done.1
  25.1 0.0 copy-done.2
  25.1 10.8 %purify.1 = f32[128,256]{1,0:T(8,128)} custom-call(f32[8,136,128]{2,1,0:T(8,128)S(1)} %pad_maximum_fusion.refs_0_, f32[16,136,128]{2,1,0:T(8,128)S(1)} %constant_dynamic-update-slice_fusion.refs_1_, f32[8,136,128]{2,1,0:T(8,128)S(1)} %pad_maximum_fusion.2.refs_2_, s32[16,9]{1,0:T(8,128)S(1)} %copy-done.1, s32[1,16]{1,0:T(1,128)S(1)} %bitcast.9), custom_call_target="tpu_custom_call" | custom-call | tf_op jit(solution)/shard_map/purify/pallas_call | solution.py:299
  (13 shorter events, 0.3 us)
Async XLA Ops:
  0.0 0.9 %copy-start = (f32[128,256]{1,0:T(8,128)S(1)}, f32[128,256]{1,0:T(8,128)}, u32[]{:S(2)}) copy-start(f32[128,256]{1,0:T(8,128)} %x_ref.1) | copy-start | bytes 393220
  0.9 7.3 %collective-permute-start.1 = (f32[136,128]{1,0:T(8,128)S(1)}, f32[136,128]{1,0:T(8,128)S(1)}, u32[]{:S(2)}, u32[]{:S(2)}) collective-permute-start(f32[136,128]{1,0:T(8,128)S(1)} %pack.1), channel_id=1, source_target_pairs={{0,16},{1,17},{2,18},{3,19},{4,20},{5,21},{6,22},{7,23},{8,24},{9,... | collective-permute-start | bytes 208904 | tf_op jit(solution)/shard_map/ppermute | solution.py:271
  4.9 4.3 %collective-permute-start.4 = (f32[136,128]{1,0:T(8,128)S(1)}, f32[136,128]{1,0:T(8,128)S(1)}, u32[]{:S(2)}, u32[]{:S(2)}) collective-permute-start(f32[136,128]{1,0:T(8,128)S(1)} %pack.1), channel_id=1, source_target_pairs={{0,8},{1,9},{2,10},{3,11},{4,12},{5,13},{6,14},{7,15},{8,0},{9,1},... | collective-permute-start | bytes 208904 | tf_op jit(solution)/shard_map/ppermute | solution.py:271
  6.5 6.1 %collective-permute-start.8 = (f32[136,128]{1,0:T(8,128)S(1)}, f32[136,128]{1,0:T(8,128)S(1)}, u32[]{:S(2)}, u32[]{:S(2)}) collective-permute-start(f32[136,128]{1,0:T(8,128)S(1)} %pack.1), channel_id=1, source_target_pairs={{0,24},{1,25},{2,26},{3,27},{4,28},{5,29},{6,30},{7,31},{8,16},{9,... | collective-permute-start | bytes 208904 | tf_op jit(solution)/shard_map/ppermute | solution.py:271
  6.5 7.6 %collective-permute-start = (f32[1,136,128]{2,1,0:T(8,128)S(1)}, f32[1,136,128]{2,1,0:T(8,128)S(1)}, u32[]{:S(2)}, u32[]{:S(2)}) collective-permute-start(f32[1,136,128]{2,1,0:T(8,128)S(1)} %bitcast.7), channel_id=1, source_target_pairs={{0,4},{1,3},{2,6},{3,1},{4,0},{5,7},{6,2},{7,5},{8,12},{9,11},{10,... | collective-permute-start | bytes 208904 | tf_op jit(solution)/shard_map/ppermute | solution.py:271
  9.3 6.5 %collective-permute-start.5 = (f32[2,136,128]{2,1,0:T(8,128)S(1)}, f32[2,136,128]{2,1,0:T(8,128)S(1)}, u32[]{:S(2)}, u32[]{:S(2)}) collective-permute-start(f32[2,136,128]{2,1,0:T(8,128)S(1)} %pad_maximum_fusion.7), channel_id=1, source_target_pairs={{0,2},{1,5},{2,0},{3,7},{4,6},{5,1},{6,4},{7,3},{8,10},{9,13},{10,... | collective-permute-start | bytes 417800 | tf_op jit(solution)/shard_map/ppermute | solution.py:271
  12.6 4.4 %collective-permute-start.9 = (f32[1,136,128]{2,1,0:T(8,128)S(1)}, f32[1,136,128]{2,1,0:T(8,128)S(1)}, u32[]{:S(2)}, u32[]{:S(2)}) collective-permute-start(f32[1,136,128]{2,1,0:T(8,128)S(1)} %bitcast.16), channel_id=1, source_target_pairs={{0,4},{1,3},{2,6},{3,1},{4,0},{5,7},{6,2},{7,5},{8,12},{9,11},{10,... | collective-permute-start | bytes 208904 | tf_op jit(solution)/shard_map/ppermute | solution.py:271
  14.1 6.5 %collective-permute-start.2 = (f32[2,136,128]{2,1,0:T(8,128)S(1)}, f32[2,136,128]{2,1,0:T(8,128)S(1)}, u32[]{:S(2)}, u32[]{:S(2)}) collective-permute-start(f32[2,136,128]{2,1,0:T(8,128)S(1)} %pad_maximum_fusion.6), channel_id=1, source_target_pairs={{0,2},{1,5},{2,0},{3,7},{4,6},{5,1},{6,4},{7,3},{8,10},{9,13},{10,... | collective-permute-start | bytes 417800 | tf_op jit(solution)/shard_map/ppermute | solution.py:271
  15.9 6.6 %collective-permute-start.6 = (f32[4,136,128]{2,1,0:T(8,128)S(1)}, f32[4,136,128]{2,1,0:T(8,128)S(1)}, u32[]{:S(2)}, u32[]{:S(2)}) collective-permute-start(f32[4,136,128]{2,1,0:T(8,128)S(1)} %pad_maximum_fusion.4), channel_id=1, source_target_pairs={{0,4},{1,3},{2,6},{3,1},{4,0},{5,7},{6,2},{7,5},{8,12},{9,11},{10,... | collective-permute-start | bytes 835592 | tf_op jit(solution)/shard_map/ppermute | solution.py:271
  17.0 5.6 %collective-permute-start.10 = (f32[2,136,128]{2,1,0:T(8,128)S(1)}, f32[2,136,128]{2,1,0:T(8,128)S(1)}, u32[]{:S(2)}, u32[]{:S(2)}) collective-permute-start(f32[2,136,128]{2,1,0:T(8,128)S(1)} %pad_maximum_fusion.8), channel_id=1, source_target_pairs={{0,2},{1,5},{2,0},{3,7},{4,6},{5,1},{6,4},{7,3},{8,10},{9,13},{10,... | collective-permute-start | bytes 417800 | tf_op jit(solution)/shard_map/ppermute | solution.py:271
  20.7 2.6 %collective-permute-start.3 = (f32[4,136,128]{2,1,0:T(8,128)S(1)}, f32[4,136,128]{2,1,0:T(8,128)S(1)}, u32[]{:S(2)}, u32[]{:S(2)}) collective-permute-start(f32[4,136,128]{2,1,0:T(8,128)S(1)} %pad_maximum_fusion.3), channel_id=1, source_target_pairs={{0,1},{1,0},{2,3},{3,2},{4,5},{5,4},{6,7},{7,6},{8,9},{9,8},{10,11... | collective-permute-start | bytes 835592 | tf_op jit(solution)/shard_map/ppermute | solution.py:271
  22.5 2.5 %collective-permute-start.7 = (f32[8,136,128]{2,1,0:T(8,128)S(1)}, f32[8,136,128]{2,1,0:T(8,128)S(1)}, u32[]{:S(2)}, u32[]{:S(2)}) collective-permute-start(f32[8,136,128]{2,1,0:T(8,128)S(1)} %pad_maximum_fusion.1), channel_id=1, source_target_pairs={{0,1},{1,0},{2,3},{3,2},{4,5},{5,4},{6,7},{7,6},{8,9},{9,8},{10,11... | collective-permute-start | bytes 1671176 | tf_op jit(solution)/shard_map/ppermute | solution.py:271
  22.6 2.3 %collective-permute-start.11 = (f32[4,136,128]{2,1,0:T(8,128)S(1)}, f32[4,136,128]{2,1,0:T(8,128)S(1)}, u32[]{:S(2)}, u32[]{:S(2)}) collective-permute-start(f32[4,136,128]{2,1,0:T(8,128)S(1)} %pad_maximum_fusion.5), channel_id=1, source_target_pairs={{0,1},{1,0},{2,3},{3,2},{4,5},{5,4},{6,7},{7,6},{8,9},{9,8},{10,11... | collective-permute-start | bytes 835592 | tf_op jit(solution)/shard_map/ppermute | solution.py:271
  23.3 1.8 %copy-start.1 = (s32[16,9]{1,0:T(8,128)S(1)}, s32[16,9]{1,0:T(8,128)}, u32[]{:S(2)}) copy-start(s32[16,9]{1,0:T(8,128)} %refs_3_.1) | copy-start | bytes 1732
  23.3 1.8 %copy-start.2 = (s32[16]{0:T(128)S(1)}, s32[16]{0:T(128)}, u32[]{:S(2)}) copy-start(s32[16]{0:T(128)} %param.5) | copy-start | bytes 196
